TPU v7x, 32 devices: a whole 2x2x4 slice. The times are simulated.
32 devices in a mesh: dp: 16 (over z, y, x), tensor: 2 (over core).
Axes of the slice: x: 2, y: 2, z: 4, core: 2. Of those that a mesh axis runs over, the one named last changes fastest.
Arguments:
- inputs: bfloat16 [16384, 768], P('dp'), may hold values from -6 to 6
- seq_lengths: int32 [16, 8], P('dp'), may hold values from 0 to 1024, as said below
- qkv_weight: bfloat16 [3, 768, 768], P(None, None, 'tensor'), may hold values from -0.21875 to 0.21875
- out_weight: bfloat16 [768, 768], P('tensor'), may hold values from -1.75 to 1.75
- up_weight: bfloat16 [768, 3072], P(None, 'tensor'), may hold values from -0.21875 to 0.21875
- down_weight: bfloat16 [3072, 768], P('tensor'), may hold values from -0.109375 to 0.109375
- select_weight: bfloat16 [2, 768, 64], replicated, may hold values from -0.079589844 to 0.079589844
- norm_gains: float32 [2, 768], replicated, may hold values from 0.5 to 1.5
- grad_output: bfloat16 [16384, 768], P('dp'), may hold values from -6 to 6
Outputs:
- output: bfloat16 [16384, 768], P('dp')
- grad_inputs: float32 [16384, 768], P('dp')
- grad_qkv: float32 [3, 768, 768], P(None, None, 'tensor')
- grad_out: float32 [768, 768], P('tensor')
- grad_up: float32 [768, 3072], P(None, 'tensor')
- grad_down: float32 [3072, 768], P('tensor')
- grad_select: float32 [2, 768, 64], replicated
- grad_gains: float32 [2, 768], replicated
Inputs may be any that keep to these rules, and one draw needn't show every extreme that they name: `seq_lengths`: each row lists up to 8 sequences packed in order into one dp index's 1024 slots: every length is a multiple of 128, zeros stand only after the last sequence, the first is at least 128, a row sums to 512 or more and at most 1024; some row holds a single sequence of 1024.
All inputs are finite; a program needn't handle non-finite values.
Results may differ from a plain program's by a relative error of at most 0.015.
The roundings to bfloat16 on the way count: a program that leaves them out, or rounds other values in their place, can miss the bound.
Values may be sent and summed in bfloat16 or wider, within the bound.
No kernel may reach another device: no remote copies, remote signals or barrier semaphores. Data moves between devices by JAX's collectives and lax.ppermute only.
A program may use at most 192 MiB of HBM per device.

v0:
```python
import functools

import jax
import jax.numpy as jnp
from jax import lax
from jax.experimental import pallas as pl
from jax.experimental.pallas import tpu as pltpu
from jax.sharding import PartitionSpec as P

BF = jnp.bfloat16
F32 = jnp.float32
EPS = 1e-6
BLK = 256
NOT_ATTENDED = 1e30
CURVE = 0.7978845608028654
CUBE = 0.044715
MIB = 1024 * 1024
COST = 1.0

DOWN = (0, 1, 2, 3), (1, 2, 0, 3)
UP = (2, 0, 1, 3), (1, 2, 0, 3)
ATT = (0, 1, 2, 3), (2, 0, 1, 3)
EARLY = "d"
LATE = "udnduabduafdugadaugdaugaddaaDuugggAU"
FREE = True


def mm(a, b):
    return jnp.dot(a, b, preferred_element_type=F32)


def mm_nt(a, b):
    return lax.dot_general(a, b, (((1,), (1,)), ((), ())), preferred_element_type=F32)


def mm_tn(a, b):
    return lax.dot_general(a, b, (((0,), (0,)), ((), ())), preferred_element_type=F32)


def params(limit_mib=56):
    return pltpu.CompilerParams(
        dimension_semantics=("arbitrary",), vmem_limit_bytes=limit_mib * MIB
    )


def cost(flops, nbytes, trans=0):
    return pl.CostEstimate(
        flops=int(COST * flops), bytes_accessed=int(COST * nbytes), transcendentals=int(COST * trans)
    )


def shape(dims, dtype):
    return jax.ShapeDtypeStruct(tuple(dims), dtype)


def whole(*dims):
    return pl.BlockSpec(tuple(dims), lambda *_: (0,) * len(dims))


def rows(width, count=BLK):
    return pl.BlockSpec((count, width), lambda i, *_: (i, 0))


def smem():
    return pl.BlockSpec(memory_space=pltpu.SMEM)


def sequence_ids(lens, pos):
    seg = jnp.zeros(pos.shape, jnp.int32)
    first = jnp.zeros(pos.shape, jnp.bool_)
    end = jnp.int32(0)
    for s in range(lens.shape[1]):
        length = lens[0, s]
        first = first | ((pos == end) & (length > 0))
        end = end + length
        seg = seg + (pos >= end).astype(jnp.int32)
    seg = jnp.where(pos < end, seg, lens.shape[1] + 1 + pos)
    return seg, first


def split_dot(values, ones):
    high = values.astype(BF)
    low = (values - high.astype(F32)).astype(BF)
    return mm(high, ones) + mm(low, ones)


def norm_scale(values):
    return lax.rsqrt(jnp.mean(values * values, axis=-1, keepdims=True) + EPS)


def rows_of(i):
    return pl.ds(pl.multiple_of(i * BLK, BLK), BLK)


def triangle(later):
    first = lax.broadcasted_iota(jnp.int32, (BLK, BLK), 0)
    second = lax.broadcasted_iota(jnp.int32, (BLK, BLK), 1)
    return jnp.where(first > second if later else first < second, 1.0, 0.0).astype(BF)


def forward_kernel(
    heads, lens, x, gains, wqkv, wsel_t, wout,
    h1_o, q_o, k_o, v_o, sq_o, sk_o, pen_o, lse_o, mix_o, part_o,
    k_s, vt_s, sk_s, carry_s, qx_s, seg_s, top_s, sum_s, acc_s,
):
    step = pl.program_id(0)
    hd = wsel_t.shape[1]
    t = k_s.shape[0]
    two = 2 * hd
    pairs = heads // 2
    scale = hd**-0.5
    here = rows_of(step)

    @pl.when(step == 0)
    def _():
        carry_s[...] = jnp.zeros_like(carry_s)
        qx_s[...] = jnp.zeros_like(qx_s)
        sk_s[...] = jnp.zeros_like(sk_s)
        seg, first = sequence_ids(lens, lax.broadcasted_iota(jnp.int32, (t, 1), 0))
        seg_s[:, 0:1] = seg
        seg_s[:, 1:2] = jnp.where(first, -1, seg)

    xf = x[...].astype(F32)
    h1 = (xf * norm_scale(xf) * gains[0:1, :]).astype(BF)
    h1_o[...] = h1
    q32 = mm(h1, wqkv[0])
    q = (q32.astype(BF) * scale).astype(BF)
    q_t = (q32.T.astype(BF) * scale).astype(BF)
    k = mm(h1, wqkv[1]).astype(BF)
    v32 = mm(h1, wqkv[2])
    sq = (mm_nt(h1, wsel_t[0]).astype(BF) * scale).astype(BF)
    sk = mm_nt(h1, wsel_t[1]).astype(BF)
    q_o[...] = q
    k_o[...] = k
    v_o[...] = v32.astype(BF)
    sq_o[...] = sq
    sk_o[...] = sk
    k_s[here, :] = k
    sk_s[here, :] = sk
    vt_s[:, here] = v32.T.astype(BF)
    for p in range(pairs):
        for side in range(2):
            h = 2 * p + side
            qx_s[p, side * hd : (side + 1) * hd, side * BLK : (side + 1) * BLK] = q_t[
                h * hd : (h + 1) * hd, :
            ]

    row = step * BLK + lax.broadcasted_iota(jnp.int32, (1, BLK), 1)
    col = lax.broadcasted_iota(jnp.int32, (t, 1), 0)
    seg_i, _ = sequence_ids(lens, row)
    sel = jnp.maximum(mm_nt(sk_s[...], sq), 0.0)
    picked = jnp.where((seg_s[:, 1:2] == seg_i) & (col < row), sel * sel, 0.0)
    pen = split_dot(picked, triangle(False)) + carry_s[:, 0:1]
    carry_s[:, 0:1] = pen[:, BLK - 1 : BLK] + picked[:, BLK - 1 : BLK]
    pen_o[...] = jnp.where((seg_s[:, 0:1] == seg_i) & (col <= row), pen, NOT_ATTENDED)

    top_s[...] = jnp.full_like(top_s, -NOT_ATTENDED)
    sum_s[...] = jnp.zeros_like(sum_s)
    acc_s[...] = jnp.zeros_like(acc_s)

    def tile(j, _):
        at = rows_of(j)
        bias = pen_o[at, :]
        bias = jnp.concatenate([bias, bias], axis=1)
        for p in range(pairs):
            s = mm(k_s[at, p * two : (p + 1) * two], qx_s[p]) - bias
            old = top_s[p : p + 1, :]
            top = jnp.maximum(old, jnp.max(s, axis=0, keepdims=True))
            fade = jnp.exp(old - top)
            prob = jnp.exp(s - top)
            top_s[p : p + 1, :] = top
            sum_s[p : p + 1, :] = sum_s[p : p + 1, :] * fade + jnp.sum(prob, axis=0, keepdims=True)
            low = prob.astype(BF)
            for side in range(2):
                mine = slice((2 * p + side) * hd, (2 * p + side + 1) * hd)
                cut = slice(side * BLK, (side + 1) * BLK)
                acc_s[mine, :] = acc_s[mine, :] * fade[:, cut] + mm(vt_s[mine, at], low[:, cut])
        return 0

    lax.fori_loop(0, step + 1, tile, 0)
    for h in range(heads):
        p, cut = h // 2, slice((h % 2) * BLK, (h % 2 + 1) * BLK)
        total = sum_s[p : p + 1, cut]
        lse_o[h : h + 1, :] = top_s[p : p + 1, cut] + jnp.log(total)
        acc_s[h * hd : (h + 1) * hd, :] = acc_s[h * hd : (h + 1) * hd, :] / total
    mixed = acc_s[...].T.astype(BF)
    mix_o[...] = mixed
    part_o[...] = mm(mixed, wout[...]).astype(BF)


def forward(lens, x, gains, wqkv, wsel_t, wout):
    t, d = x.shape
    wh = wqkv.shape[2]
    hd = wsel_t.shape[1]
    heads = wh // hd
    n = t // BLK
    tall = pl.BlockSpec((t, BLK), lambda i: (0, i))
    return pl.pallas_call(
        functools.partial(forward_kernel, heads),
        grid=(n,),
        in_specs=[
            smem(), rows(d), whole(*gains.shape), whole(*wqkv.shape), whole(*wsel_t.shape),
            whole(*wout.shape),
        ],
        out_specs=[
            rows(d), rows(wh), rows(wh), rows(wh), rows(hd), rows(hd), tall,
            pl.BlockSpec((8, BLK), lambda i: (0, i)), rows(wh), rows(d),
        ],
        out_shape=[
            shape((t, d), BF), shape((t, wh), BF), shape((t, wh), BF), shape((t, wh), BF),
            shape((t, hd), BF), shape((t, hd), BF), shape((t, t), F32), shape((8, t), F32),
            shape((t, wh), BF), shape((t, d), BF),
        ],
        scratch_shapes=[
            pltpu.VMEM((t, wh), BF), pltpu.VMEM((wh, t), BF), pltpu.VMEM((t, hd), BF),
            pltpu.VMEM((t, 128), F32), pltpu.VMEM((heads // 2, 2 * hd, 2 * BLK), BF),
            pltpu.VMEM((t, 128), jnp.int32), pltpu.VMEM((8, 2 * BLK), F32),
            pltpu.VMEM((8, 2 * BLK), F32), pltpu.VMEM((wh, BLK), F32),
        ],
        compiler_params=params(),
        cost_estimate=cost(2 * t * d * (4 * wh + 2 * hd) + 4 * heads * t * t * hd, 16 * MIB, heads * t * t),
        name="attention_forward",
    )(lens, x, gains, wqkv, wsel_t, wout)


def feed_kernel(
    half, x, part_a, part_b, gains, up, down, g, mid_o, h2_o, act_o, du_o, dn_o, dsend_o,
    act_s,
):
    step = pl.program_id(0)
    here = rows_of(step)
    mid = x[...].astype(F32) + (part_a[...].astype(F32) + part_b[...].astype(F32))
    mid_o[...] = mid
    h2 = (mid * norm_scale(mid) * gains[1:2, :]).astype(BF)
    h2_o[...] = h2
    hidden = up.shape[1]
    chunk = 512
    dn = jnp.zeros(mid.shape, F32)
    for c in range(hidden // chunk):
        cut = slice(c * chunk, (c + 1) * chunk)
        u = mm(h2, up[:, cut])
        da = mm_nt(g[here, :], down[cut, :])
        u2 = u * u
        curve = jnp.tanh(u * (CURVE + (CURVE * CUBE) * u2))
        part = 0.5 * (1.0 + curve)
        act = (u * part).astype(BF)
        slope = part + (0.5 * u) * (1.0 - curve * curve) * (CURVE + (3.0 * CURVE * CUBE) * u2)
        du = (da * slope).astype(BF)
        act_o[:, cut] = act
        act_s[here, cut] = act
        du_o[:, cut] = du
        dn = dn + mm_nt(du, up[:, cut])
    dn_o[...] = dn.astype(BF)

    @pl.when(step == pl.num_programs(0) - 1)
    def _():
        tile = 128
        for j in range(dsend_o.shape[0] // tile):
            at = pl.ds(pl.multiple_of(half[0] * dsend_o.shape[0] + j * tile, tile), tile)
            dsend_o[j * tile : (j + 1) * tile, :] = mm_tn(act_s[:, at], g[...]).astype(BF)


def feed(half, x, part_a, part_b, gains, up, down, g):
    t, d = x.shape
    hidden = up.shape[1]
    return pl.pallas_call(
        feed_kernel,
        grid=(t // BLK,),
        in_specs=[
            smem(), rows(d), rows(d), rows(d), whole(*gains.shape), whole(*up.shape),
            whole(*down.shape), whole(t, d),
        ],
        out_specs=[
            rows(d), rows(d), rows(hidden), rows(hidden), rows(d), whole(hidden // 2, d),
        ],
        out_shape=[
            shape((t, d), F32), shape((t, d), BF), shape((t, hidden), BF), shape((t, hidden), BF),
            shape((t, d), BF), shape((hidden // 2, d), BF),
        ],
        scratch_shapes=[pltpu.VMEM((t, hidden), BF)],
        compiler_params=params(),
        cost_estimate=cost(8 * t * d * hidden, 24 * MIB, t * hidden),
        name="feed_forward",
    )(half, x, part_a, part_b, gains, up, down, g)


def product_kernel(half, left, right, out):
    out[...] = mm_tn(left[...], right[...]).astype(BF)


def down_half(half, act, g):
    t, hidden = act.shape
    d = g.shape[1]
    tiles = 3
    tile = hidden // 2 // tiles
    return pl.pallas_call(
        product_kernel,
        grid_spec=pltpu.PrefetchScalarGridSpec(
            num_scalar_prefetch=1,
            grid=(tiles,),
            in_specs=[
                pl.BlockSpec((t, tile), lambda j, half: (0, half[0] * tiles + j)),
                whole(t, d),
            ],
            out_specs=pl.BlockSpec((tile, d), lambda j, half: (j, 0)),
        ),
        out_shape=shape((hidden // 2, d), BF),
        compiler_params=params(),
        cost_estimate=cost(t * d * hidden, 6 * MIB),
        name="grad_down",
    )(half, act, g)


def norm_back(values, scale, gain, grad):
    unit = values * scale
    grad_unit = grad * gain
    mean = jnp.mean(grad_unit * unit, axis=-1, keepdims=True)
    return scale * (grad_unit - unit * mean), jnp.sum(grad * unit, axis=0, keepdims=True)


def middle_kernel(
    hd, half, mid, part_a, part_b, gains, g, wout, mixed, h2, du, dmid_o, gm_o, dmix_o, dots_o,
    send_o, keep_o, gain_o, gm_s,
):
    step = pl.program_id(0)
    here = rows_of(step)
    values = mid[...]
    grad = part_a[...].astype(F32) + part_b[...].astype(F32)
    back, gain_grad = norm_back(values, norm_scale(values), gains[1:2, :], grad)
    dmid = g[...].astype(F32) + back
    dmid_o[...] = dmid
    gm = dmid.astype(BF)
    gm_o[...] = gm
    gm_s[here, :] = gm
    dmix = mm_nt(gm, wout[...]).astype(BF)
    dmix_o[...] = dmix
    both = (dmix.astype(F32) * mixed[here, :].astype(F32)).T
    for h in range(both.shape[0] // hd):
        dots_o[h : h + 1, :] = jnp.sum(both[h * hd : (h + 1) * hd, :], axis=0, keepdims=True)

    @pl.when(step == 0)
    def _():
        gain_o[...] = jnp.zeros_like(gain_o)

    gain_o[0:1, :] += gain_grad

    @pl.when(step == pl.num_programs(0) - 1)
    def _():
        hidden = du.shape[1]
        size = send_o.shape[0]
        tile = 128
        for which, into in ((half[0], send_o), (1 - half[0], keep_o)):
            half_at = pl.multiple_of(which * size, tile)
            for r in range(size // tile):
                out = slice(r * tile, (r + 1) * tile)
                at = pl.ds(pl.multiple_of(half_at + r * tile, tile), tile)
                into[out, :hidden] = mm_tn(h2[:, at], du[...]).astype(BF)
                into[out, hidden:] = mm_tn(mixed[:, out], gm_s[:, pl.ds(half_at, size)]).astype(BF)


def middle(half, mid, part_a, part_b, gains, g, wout, mixed, h2, du, hd):
    t, d = mid.shape
    wh = wout.shape[0]
    hidden = du.shape[1]
    return pl.pallas_call(
        functools.partial(middle_kernel, hd),
        grid=(t // BLK,),
        in_specs=[
            smem(), rows(d), rows(d), rows(d), whole(*gains.shape), rows(d), whole(*wout.shape),
            whole(t, wh), whole(t, d), whole(t, hidden),
        ],
        out_specs=[
            rows(d), rows(d), rows(wh), pl.BlockSpec((8, BLK), lambda i: (0, i)),
            whole(d // 2, hidden + d // 2), whole(d // 2, hidden + d // 2), whole(8, d),
        ],
        out_shape=[
            shape((t, d), F32), shape((t, d), BF), shape((t, wh), BF), shape((8, t), F32),
            shape((d // 2, hidden + d // 2), BF), shape((d // 2, hidden + d // 2), BF),
            shape((8, d), F32),
        ],
        scratch_shapes=[pltpu.VMEM((t, d), BF)],
        compiler_params=params(),
        cost_estimate=cost(2 * t * d * wh + t * d * hidden, 20 * MIB),
        name="second_norm_backward",
    )(half, mid, part_a, part_b, gains, g, wout, mixed, h2, du)


def split_three(values):
    one = values.astype(BF).astype(F32)
    rest = values - one
    two = rest.astype(BF).astype(F32)
    return one, two, (rest - two).astype(BF).astype(F32)


def backward_kernel(
    n_blocks, heads, lens, half, q, k, v, sq, sk, pen, lse, dots, dmix, h1, cat_o, send_o, keep_o,
    qx_s, qm_s, dx_s, dm_s, dq_s, dsq_s, dk_s, dv_s, dsk_s, kt_s, skt_s, kx_s, vx_s, seg_s,
):
    j = pl.program_id(0)
    wh = k.shape[1]
    hd = sk.shape[1]
    t = q.shape[0]
    two = 2 * hd
    pairs = heads // 2
    scale = hd**-0.5
    lane = lax.broadcasted_iota(jnp.int32, (1, two), 1)
    side_of = [lane // hd == side for side in range(2)]
    ones = jnp.broadcast_to(jnp.where(lane < 3, 1.0, 0.0).astype(BF), (BLK, two))

    @pl.when(j == 0)
    def _():
        dq_s[...] = jnp.zeros_like(dq_s)
        dsq_s[...] = jnp.zeros_like(dsq_s)
        seg, _ = sequence_ids(lens, lax.broadcasted_iota(jnp.int32, (1, t), 1))
        seg_s[0:1, :] = seg

        tall = lax.broadcasted_iota(jnp.int32, (two, 1), 0)

        def prepare(i, _):
            at = rows_of(i)
            for which, (source, plain, wide) in enumerate(((q, qm_s, qx_s), (dmix, dm_s, dx_s))):
                source_t = source[at, :].astype(F32).T
                for h in range(heads):
                    side = h % 2
                    pair = slice((h // 2) * two, (h // 2 + 1) * two)
                    cut = slice(side * BLK, (side + 1) * BLK)
                    value = jnp.where(side_of[side], source[at, pair], jnp.zeros((), BF))
                    plain[h // 2, i, cut, :] = value
                    value = jnp.where(tall // hd == side, source_t[pair, :], 0.0)
                    wide[h // 2, i, 0:two, cut] = value.astype(BF)
                    one, mid, low = split_three(-(lse, dots)[which][h : h + 1, at])
                    value = jnp.where(tall == 0, one, jnp.where(tall == 1, mid, jnp.where(tall == 2, low, 0.0)))
                    wide[h // 2, i, two : 2 * two, cut] = value.astype(BF)
            return 0

        lax.fori_loop(0, n_blocks, prepare, 0)

    here = rows_of(j)
    dk_s[...] = jnp.zeros_like(dk_s)
    dv_s[...] = jnp.zeros_like(dv_s)
    dsk_s[...] = jnp.zeros_like(dsk_s)
    kt_s[...] = k[...].astype(F32).T.astype(BF)
    skt_s[...] = sk[...].astype(F32).T.astype(BF)
    for p in range(pairs):
        pair = slice(p * two, (p + 1) * two)
        kx_s[p, :, 0:two] = k[:, pair]
        vx_s[p, :, 0:two] = v[:, pair]
        kx_s[p, :, two:] = ones
        vx_s[p, :, two:] = ones
    after = triangle(True)
    col = j * BLK + lax.broadcasted_iota(jnp.int32, (BLK, 1), 0)
    seg_j, first_j = sequence_ids(lens, col)
    seg_j = jnp.where(first_j, -1, seg_j)

    def tile(back, carry):
        i = n_blocks - 1 - back
        at = rows_of(i)
        bias = pen[:, at]
        dpen = None
        for p in range(pairs):
            pair = slice(p * two, (p + 1) * two)
            prob = jnp.exp(mm(kx_s[p], qx_s[p, i]) - jnp.concatenate([bias, bias], axis=1))
            dscore = prob * mm(vx_s[p], dx_s[p, i])
            both = dscore[:, :BLK] + dscore[:, BLK:]
            dpen = both if dpen is None else dpen + both
            low = dscore.astype(BF)
            for side in range(2):
                h = 2 * p + side
                dq_s[p, side * hd : (side + 1) * hd, at] += mm(
                    kt_s[h * hd : (h + 1) * hd, :], low[:, side * BLK : (side + 1) * BLK]
                )
            dv_s[:, pair] += mm(prob.astype(BF), dm_s[p, i])
            dk_s[:, pair] += mm(low, qm_s[p, i])
        dpicked = split_dot(dpen, after) + carry
        row = i * BLK + lax.broadcasted_iota(jnp.int32, (1, BLK), 1)
        chosen = (seg_j == seg_s[0:1, at]) & (col < row)
        sel = jnp.maximum(mm_nt(sk[...], sq[at, :]), 0.0)
        dsel = jnp.where(chosen, -2.0 * dpicked * sel, 0.0).astype(BF)
        dsk_s[...] += mm(dsel, sq[at, :])
        dsq_s[:, at] += mm(skt_s[...], dsel)
        return dpicked[:, 0:1] + dpen[:, 0:1]

    lax.fori_loop(0, n_blocks - j, tile, jnp.zeros((BLK, 1), F32))
    cat_o[here, wh : 2 * wh] = dk_s[...].astype(BF)
    cat_o[here, 2 * wh : 3 * wh] = dv_s[...].astype(BF)
    cat_o[here, 3 * wh + hd : 3 * wh + 2 * hd] = dsk_s[...].astype(BF)

    @pl.when(j == n_blocks - 1)
    def _():
        for p in range(pairs):
            cat_o[:, p * two : (p + 1) * two] = (dq_s[p] * scale).T.astype(BF)
        cat_o[:, 3 * wh : 3 * wh + hd] = (dsq_s[...] * scale).T.astype(BF)
        size = send_o.shape[0]
        tile = 128
        for which, into in ((half[0], send_o), (1 - half[0], keep_o)):
            for r in range(size // tile):
                at = pl.ds(pl.multiple_of(which * size + r * tile, tile), tile)
                into[r * tile : (r + 1) * tile, :] = mm_tn(h1[:, at], cat_o[...]).astype(BF)


def backward(lens, half, q, k, v, sq, sk, pen, lse, dots, dmix, h1):
    d = h1.shape[1]
    t, wh = q.shape
    hd = sq.shape[1]
    heads = wh // hd
    n = t // BLK
    width = 3 * wh + 2 * hd
    per_head = pltpu.VMEM((heads // 2, n, 2 * BLK, 2 * hd), BF)
    per_head_t = pltpu.VMEM((heads // 2, n, 4 * hd, 2 * BLK), BF)
    return pl.pallas_call(
        functools.partial(backward_kernel, n, heads),
        grid=(n,),
        in_specs=[
            smem(), smem(), whole(t, wh), rows(wh), rows(wh), whole(t, hd), rows(hd), rows(t),
            whole(8, t), whole(8, t), whole(t, wh), whole(t, d),
        ],
        out_specs=[whole(t, width), whole(d // 2, width), whole(d // 2, width)],
        out_shape=[
            shape((t, width), BF), shape((d // 2, width), BF), shape((d // 2, width), BF),
        ],
        scratch_shapes=[
            per_head_t, per_head, per_head_t, per_head, pltpu.VMEM((heads // 2, 2 * hd, t), F32),
            pltpu.VMEM((hd, t), F32), pltpu.VMEM((BLK, wh), F32),
            pltpu.VMEM((BLK, wh), F32), pltpu.VMEM((BLK, hd), F32), pltpu.VMEM((wh, BLK), BF),
            pltpu.VMEM((hd, BLK), BF), pltpu.VMEM((heads // 2, BLK, 4 * hd), BF),
            pltpu.VMEM((heads // 2, BLK, 4 * hd), BF), pltpu.VMEM((8, t), jnp.int32),
        ],
        compiler_params=params(),
        cost_estimate=cost(10 * heads * t * t * hd, 12 * MIB, heads * t * t),
        name="attention_backward",
    )(lens, half, q, k, v, sq, sk, pen, lse, dots, dmix, h1)


def first_kernel(cat, wqkv, wsel, out):
    wh = wqkv.shape[2]
    total = mm(cat[:, 3 * wh :], wsel[...])
    for i in range(3):
        total = total + mm_nt(cat[:, i * wh : (i + 1) * wh], wqkv[i])
    out[...] = total.astype(BF)


def first_grad(cat, wqkv, wsel):
    t, width = cat.shape
    d = wqkv.shape[1]
    return pl.pallas_call(
        first_kernel,
        grid=(t // BLK,),
        in_specs=[rows(width), whole(*wqkv.shape), whole(*wsel.shape)],
        out_specs=rows(d),
        out_shape=shape((t, d), BF),
        compiler_params=params(),
        cost_estimate=cost(2 * t * d * width, 6 * MIB),
        name="first_norm_grad",
    )(cat, wqkv, wsel)


def finish_kernel(
    x, part_a, part_b, gains, dmid, mid, fold_a, fold_b, grad_o, out_o, gain_o
):
    values = x[...].astype(F32)
    grad = part_a[...].astype(F32) + part_b[...].astype(F32)
    back, gain_grad = norm_back(values, norm_scale(values), gains[0:1, :], grad)
    grad_o[...] = dmid[...] + back
    out_o[...] = (mid[...] + (fold_a[...].astype(F32) + fold_b[...].astype(F32))).astype(BF)

    @pl.when(pl.program_id(0) == 0)
    def _():
        gain_o[...] = jnp.zeros_like(gain_o)

    gain_o[0:1, :] += gain_grad


def finish(x, part_a, part_b, gains, dmid, mid, fold_a, fold_b):
    t, d = x.shape
    return pl.pallas_call(
        finish_kernel,
        grid=(t // BLK,),
        in_specs=[rows(d), rows(d), rows(d), whole(*gains.shape)] + [rows(d)] * 4,
        out_specs=[rows(d), rows(d), whole(8, d)],
        out_shape=[shape((t, d), F32), shape((t, d), BF), shape((8, d), F32)],
        compiler_params=params(),
        cost_estimate=cost(24 * t * d, 20 * MIB),
        name="first_norm_backward",
    )(x, part_a, part_b, gains, dmid, mid, fold_a, fold_b)


def branch_kernel(act, down, out):
    out[...] = mm(act[...], down[...]).astype(BF)


def branch(act, down):
    t, hidden = act.shape
    d = down.shape[1]
    return pl.pallas_call(
        branch_kernel,
        grid=(t // BLK,),
        in_specs=[rows(hidden), whole(*down.shape)],
        out_specs=rows(d),
        out_shape=shape((t, d), BF),
        compiler_params=params(),
        cost_estimate=cost(2 * t * d * hidden, 8 * MIB),
        name="down_projection",
    )(act, down)


class Sum:
    def __init__(self, n_dp, n_tensor, orders):
        self.n_dp, self.n_tensor = n_dp, n_tensor
        self.stages = n_dp.bit_length() - 1
        rest = list(range(4, self.stages))
        self.orders = [[1 << b for b in list(orders[t % 2]) + rest] for t in range(n_tensor)]
        self.dp = lax.axis_index("dp")
        self.tensor = lax.axis_index("tensor")

    def place(self, stage):
        out = (self.dp // self.orders[0][stage]) % 2
        for t in range(1, self.n_tensor):
            out = jnp.where(self.tensor == t, (self.dp // self.orders[t][stage]) % 2, out)
        return out

    def swap(self, value, stage):
        pairs = [
            (i * self.n_tensor + t, (i ^ self.orders[t][stage]) * self.n_tensor + t)
            for i in range(self.n_dp)
            for t in range(self.n_tensor)
        ]
        return lax.ppermute(value, ("dp", "tensor"), pairs)

    def split(self, stage, *terms):
        size = terms[0].shape[0] // 2
        place = self.place(stage)

        def cut(which):
            pieces = [lax.dynamic_slice_in_dim(v, which * size, size, 0) for v in terms]
            return (pieces[0].astype(F32) + pieces[1].astype(F32)).astype(BF)

        return [cut(1 - place), cut(place)]

    def join(self, stage, mine, other):
        place = self.place(stage)
        low, high = jnp.where(place == 0, mine, other), jnp.where(place == 0, other, mine)
        return jnp.concatenate([low, high], axis=0)


class Chain:
    def __init__(self, sums, line):
        self.sums, self.line, self.stage = sums, line, 0

    def begin(self, send):
        self.got = self.sums.swap(send, 0)

    def hold(self, keep):
        self.keep = keep

    def reduce(self):
        sums, self.stage = self.sums, self.stage + 1
        if self.stage < sums.stages:
            split = functools.partial(sums.split, self.stage)
            send, self.keep = self.line.run(split, self.keep, self.got)
            self.got = sums.swap(send, self.stage)
        else:
            add = lambda a, b: [(a.astype(F32) + b.astype(F32)).astype(BF)]
            (self.piece,) = self.line.run(add, self.keep, self.got)
            self.spread()

    def spread(self):
        self.stage -= 1
        self.got = self.sums.swap(self.piece, self.stage)

    def gather(self):
        join = lambda *v: [self.sums.join(self.stage, *v)]
        (self.piece,) = self.line.run(join, self.piece, self.got)
        self.spread()

    def step(self):
        if not hasattr(self, "piece"):
            self.reduce()
        elif self.stage > 0:
            self.gather()
        else:
            return False
        return True

    def halves(self):
        return self.piece, self.got


class Line:
    def __init__(self):
        self.token = None

    def run(self, step, *values, after=()):
        if self.token is not None:
            first, *_ = lax.optimization_barrier((values[0], self.token, *after))
            values = (first, *values[1:])
        out = step(*values)
        self.token = out[0]
        return out


def swap_tensor(value, n_tensor):
    return lax.ppermute(value, "tensor", [(t, t ^ 1) for t in range(n_tensor)])


def join_kernel(side, mine, other, out):
    @pl.when(pl.program_id(0) == 0)
    def _():
        out[...] = mine[...].astype(F32)

    @pl.when(pl.program_id(0) == 1)
    def _():
        out[...] = other[...].astype(F32)


def join(side, mine, other):
    r, n = mine.shape
    tiles = 3
    tile = r // tiles
    return pl.pallas_call(
        join_kernel,
        grid_spec=pltpu.PrefetchScalarGridSpec(
            num_scalar_prefetch=1,
            grid=(2, tiles),
            in_specs=[
                pl.BlockSpec((tile, n), lambda s, j, side: (jnp.where(s == 0, j, tiles - 1), 0)),
                pl.BlockSpec((tile, n), lambda s, j, side: (jnp.where(s == 0, 0, j), 0)),
            ],
            out_specs=pl.BlockSpec(
                (tile, n), lambda s, j, side: (jnp.where(s == 0, side[0], 1 - side[0]) * tiles + j, 0)
            ),
        ),
        out_shape=shape((2 * r, n), F32),
        compiler_params=pltpu.CompilerParams(
            dimension_semantics=("arbitrary", "arbitrary"), vmem_limit_bytes=32 * MIB
        ),
        cost_estimate=cost(0, 12 * r * n),
        name="join_halves",
    )(side, mine, other)


def join_up_kernel(side, mine, other, up_o, out_o):
    def put(piece):
        up_o[...] = piece[:, : up_o.shape[1]].astype(F32)
        out_o[...] = piece[:, up_o.shape[1] :].astype(F32)

    pl.when(pl.program_id(0) == 0)(lambda: put(mine[...]))
    pl.when(pl.program_id(0) == 1)(lambda: put(other[...]))


def join_up(side, mine, other, hidden, wh):
    r, n = mine.shape
    place = lambda s, side: jnp.where(s == 0, side[0], 1 - side[0])
    return pl.pallas_call(
        join_up_kernel,
        grid_spec=pltpu.PrefetchScalarGridSpec(
            num_scalar_prefetch=1,
            grid=(2,),
            in_specs=[pl.BlockSpec((r, n), lambda s, side: (0, 0))] * 2,
            out_specs=[
                pl.BlockSpec((r, hidden), lambda s, side: (place(s, side), 0)),
                pl.BlockSpec((wh, r), lambda s, side: (0, place(s, side))),
            ],
        ),
        out_shape=[shape((2 * r, hidden), F32), shape((wh, 2 * r), F32)],
        compiler_params=params(32),
        cost_estimate=cost(0, 12 * r * n),
        name="join_up",
    )(side, mine, other)


def join_attention_kernel(wh, side, mine, other, qkv_o, sel_o):
    def put(piece):
        for i in range(3):
            qkv_o[i] = piece[:, i * wh : (i + 1) * wh].astype(F32)
        sel_o[...] = piece[:, 3 * wh :].astype(F32)

    pl.when(pl.program_id(0) == 0)(lambda: put(mine[...]))
    pl.when(pl.program_id(0) == 1)(lambda: put(other[...]))


def join_attention(side, mine, other, wh, hd):
    r, n = mine.shape
    place = lambda s, side: jnp.where(s == 0, side[0], 1 - side[0])
    return pl.pallas_call(
        functools.partial(join_attention_kernel, wh),
        grid_spec=pltpu.PrefetchScalarGridSpec(
            num_scalar_prefetch=1,
            grid=(2,),
            in_specs=[pl.BlockSpec((r, n), lambda s, side: (0, 0))] * 2,
            out_specs=[
                pl.BlockSpec((3, r, wh), lambda s, side: (0, place(s, side), 0)),
                pl.BlockSpec((r, 2 * hd), lambda s, side: (place(s, side), 0)),
            ],
        ),
        out_shape=[shape((3, 2 * r, wh), F32), shape((2 * r, 2 * hd), F32)],
        compiler_params=params(32),
        cost_estimate=cost(0, 12 * r * n),
        name="join_attention",
    )(side, mine, other)


def per_device(
    n_dp, n_tensor, inputs, seq_lengths, qkv_weight, out_weight, up_weight, down_weight,
    select_weight, norm_gains, grad_output,
):
    wh = qkv_weight.shape[2]
    hd = select_weight.shape[2]
    d = inputs.shape[1]
    hidden = up_weight.shape[1]
    line = Line()
    run = line.run
    sums = [Sum(n_dp, n_tensor, orders) for orders in (DOWN, UP, ATT)]
    down, up, att = (Chain(each, line) for each in sums)
    small = sums[0]
    down_kept, up_kept, att_kept = (
        each.place(0).reshape(1).astype(jnp.int32) for each in sums
    )
    select_t = jnp.swapaxes(select_weight, 1, 2)
    swap = functools.partial(swap_tensor, n_tensor=n_tensor)

    h1, q, k, v, sq, sk, pen, lse, mixed, part = run(
        forward, seq_lengths, inputs, norm_gains, qkv_weight, select_t, out_weight
    )
    mid, h2, act, du, dn2, down_send = run(
        lambda part, *v: feed(1 - down_kept, inputs, part, *v),
        part, swap(part), norm_gains, up_weight, down_weight, grad_output,
    )
    dn2_other = swap(dn2)
    down.begin(down_send)
    down.hold(*run(lambda act, *v: [down_half(down_kept, act, *v)], act, grad_output))
    dmid, gm, dmix, dots, up_send, up_keep, gain_two = run(
        lambda dn2, *v: middle(1 - up_kept, mid, dn2, *v, hd),
        dn2, dn2_other, norm_gains, grad_output, out_weight, mixed, h2, du,
    )
    up.begin(up_send)
    up.hold(up_keep)
    steps = {"d": down.step, "u": up.step, "a": att.step}
    for letter in EARLY:
        steps[letter]()
    cat, att_send, att_keep = run(
        lambda dots, *v: backward(seq_lengths, 1 - att_kept, *v[:7], dots, *v[7:]),
        dots, q, k, v, sq, sk, pen, lse, dmix, h1,
    )
    att.begin(att_send)
    att.hold(att_keep)
    done = {}

    def first():
        value = (first_grad if FREE else over(first_grad))(cat, qkv_weight, select_t.reshape(2 * hd, d))
        done["dn1"] = value, swap(value)

    def fold():
        value = (branch if FREE else over(branch))(act, down_weight)
        done["fold"] = value, swap(value)

    def over(kernel):
        return lambda *v: run(lambda *w: [kernel(*w)], *v)[0]

    def last():
        done["inputs"], done["output"], gain_one = run(
            lambda dn1, *v: finish(inputs, dn1, *v),
            *done["dn1"], norm_gains, dmid, mid, *done["fold"],
        )
        done["gains"] = jnp.concatenate([gain_one[0:1], gain_two[0:1]], axis=0), 0

    def gain():
        value, stage = done["gains"]
        if stage == small.stages:
            return False
        (value,) = run(lambda *v: [v[0] + v[1]], value, small.swap(value, stage))
        done["gains"] = value, stage + 1
        return True

    def down_out():
        while down.step():
            pass
        (done["down"],) = run(lambda *v: [join(down_kept, *v)], *down.halves())

    def up_out():
        while up.step():
            pass
        done["up"] = run(lambda *v: join_up(up_kept, *v, hidden, wh), *up.halves())

    def att_out():
        while att.step():
            pass
        done["att"] = run(lambda *v: join_attention(att_kept, *v, wh, hd), *att.halves())

    steps.update(n=first, b=fold, f=last, g=gain, D=down_out, U=up_out, A=att_out)
    for letter in LATE:
        steps[letter]()
    while gain():
        pass
    grad_inputs, output, gains, grad_down = (done[k] for k in ("inputs", "output", "gains", "down"))
    gains = gains[0]
    grad_up, grad_out = done["up"]
    grad_qkv, select_part = done["att"]
    select_t_sum = select_part.T
    select_t_sum = select_t_sum + swap(select_t_sum)
    grad_select = jnp.swapaxes(select_t_sum.reshape(2, hd, d), 1, 2)
    return (output, grad_inputs, grad_qkv, grad_out, grad_up, grad_down, grad_select, gains)


def solution(mesh):
    placed = (
        P("dp", None),
        P("dp", None),
        P(None, None, "tensor"),
        P("tensor", None),
        P(None, "tensor"),
        P("tensor", None),
        P(),
        P(),
        P("dp", None),
    )
    return jax.shard_map(
        functools.partial(per_device, mesh.shape["dp"], mesh.shape["tensor"]),
        mesh=mesh,
        in_specs=placed,
        out_specs=(
            P("dp", None),
            P("dp", None),
            P(None, None, "tensor"),
            P("tensor", None),
            P(None, "tensor"),
            P("tensor", None),
            P(),
            P(),
        ),
        check_vma=False,
    )
```

profile of v0, /device:TPU:1, one launch (start us, length us, event | category | flops | bytes accessed | tf_op | source)
XLA Modules:
  0.0 242.8 jit_solution(4589900384128333157)
XLA Ops:
  0.6 25.5 %attention_forward.1 = (bf16[1024,768]{1,0:T(8,128)(2,1)}, bf16[1024,384]{1,0:T(8,128)(2,1)}, bf16[1024,384]{1,0:T(8,128)(2,1)}, bf16[1024,384]{1,0:T(8,128)(2,1...) custom-call(s32[1,8]{1,0:T(1,128)} %lens.3, ...), custom_call_target="tpu_custom_call" | custom-call | flops 4227858432 | bytes 16777216 | tf_op jit(solution)/shard_map/attention_forward/pallas_call | solution.py:198
  26.2 3.6 %collective-permute-done.part_b = bf16[1024,768]{1,0:T(8,128)(2,1)S(1)} collective-permute-done((bf16[1024,768]{1,0:T(8,128)(2,1)}, bf16[1024,768]{1,0:T(8,128)(2,1)S(1)}, u32[]{:S(2)}, u32[]{:S(2)}) %collective-permute-start) | collective-permute-done | bytes 1572896 | tf_op jit(solution)/shard_map/ppermute | solution.py:702
  30.9 17.1 %feed_forward.1 = (f32[1024,768]{1,0:T(8,128)}, bf16[1024,768]{1,0:T(8,128)(2,1)}, bf16[1024,1536]{1,0:T(8,128)(2,1)}, bf16[1024,1536]{1,0:T(8,128)(2,1)}, bf16[...) custom-call(s32[1]{0:T(128)S(6)} %sub.83.half, bf16[1024,768]{1,0:T(8,128)(2,1)} %x.5, ...), custom_call_target="tpu_custom_call" | custom-call | flops 9663676416 | bytes 25165824 | tf_op jit(solution)/shard_map/feed_forward/pallas_call | solution.py:266
  48.2 2.6 %collective-permute-start.2 = (bf16[768,768]{1,0:T(8,128)(2,1)}, bf16[768,768]{1,0:T(8,128)(2,1)}, u32[]{:S(2)}, u32[]{:S(2)}) collective-permute-start(bf16[768,768]{1,0:T(8,128)(2,1)} %get-tuple-element.94), channel_id=1, source_target_pairs={{0,2},{1,5},{2,0},{3,7},{4,6},{5,1},{6,4},{7,3},{8,10},{9,13},{10,... | collective-permute-start | bytes 3538952 | tf_op jit(solution)/shard_map/ppermute | solution.py:627
  50.8 4.8 %grad_down.1 = bf16[768,768]{1,0:T(8,128)(2,1)} custom-call(s32[1]{0:T(128)} %bitcast.3.half.side, bf16[1024,1536]{1,0:T(8,128)(2,1)} %get-tuple-element.86.left.act, bf16[1024,768]{1,0:T(8,128)(2,1)} %g.3), custom_call_target="tpu_custom_call" | custom-call | flops 1207959552 | bytes 6291456 | tf_op jit(solution)/shard_map/grad_down/pallas_call | solution.py:296
  56.8 14.3 %second_norm_backward.1 = (f32[1024,768]{1,0:T(8,128)}, bf16[1024,768]{1,0:T(8,128)(2,1)}, bf16[1024,384]{1,0:T(8,128)(2,1)}, f32[8,1024]{1,0:T(8,128)}, bf16[38...) custom-call(s32[1]{0:T(128)S(6)} %sub.82.half, f32[1024,768]{1,0:T(8,128)} %get-tuple-element.83.mid, ...), custom_call_target="tpu_custom_call" | custom-call | flops 1811939328 | bytes 20971520 | tf_op jit(solution)/shard_map/second_norm_backward/pallas_call | solution.py:365
  74.4 29.5 %attention_backward.1 = (bf16[1024,1280]{1,0:T(8,128)(2,1)}, bf16[384,1280]{1,0:T(8,128)(2,1)}, bf16[384,1280]{1,0:T(8,128)(2,1)}) custom-call(s32[1,8]{1,0:T(1,128)} %lens.3, s32[1]{0:T(128)S(6)} %sub.80.half, bf16[1024,384]{1,0:T(8,128)(2,1)} %get-tuple-element.73.q, bf16[1024,384]{1,0:T(8,128)(2,1)} %get-tuple-element.74.k, ...), custom_call_target="tpu_custom_call" | custom-call | flops 4026531840 | bytes 12582912 | tf_op jit(solution)/shard_map/attention_backward/pallas_call | solution.py:510
  107.1 6.4 %down_projection.1.fold_a = bf16[1024,768]{1,0:T(8,128)(2,1)} custom-call(bf16[1024,1536]{1,0:T(8,128)(2,1)} %get-tuple-element.86.left.act, bf16[1536,768]{1,0:T(8,128)(2,1)} %down.3), custom_call_target="tpu_custom_call" | custom-call | flops 2415919104 | bytes 8388608 | tf_op jit(solution)/shard_map/down_projection/pallas_call | solution.py:594
  113.5 2.5 %collective-permute-start.12 = (bf16[1024,768]{1,0:T(8,128)(2,1)}, bf16[1024,768]{1,0:T(8,128)(2,1)S(1)}, u32[]{:S(2)}, u32[]{:S(2)}) collective-permute-start(bf16[1024,768]{1,0:T(8,128)(2,1)} %down_projection.1.fold_a), channel_id=1, source_target_pairs={{0,1},{1,0},{2,3},{3,2},{4,5},{5,4},{6,7},{7,6},{8,9},{9,8},{10,11... | collective-permute-start | bytes 4718600 | tf_op jit(solution)/shard_map/ppermute | solution.py:702
  117.1 6.4 %first_norm_grad.1.part_a = bf16[1024,768]{1,0:T(8,128)(2,1)} custom-call(bf16[1024,1280]{1,0:T(8,128)(2,1)} %get-tuple-element.97.cat, bf16[3,768,384]{2,1,0:T(8,128)(2,1)} %wqkv.3, bf16[128,768]{1,0:T(8,128)(2,1)} %bitcast.14), custom_call_target="tpu_custom_call" | custom-call | flops 2013265920 | bytes 6291456 | tf_op jit(solution)/shard_map/first_norm_grad/pallas_call | solution.py:545
  123.7 2.5 %collective-permute-done.5 = bf16[192,768]{1,0:T(8,128)(2,1)} collective-permute-done((bf16[192,768]{1,0:T(8,128)(2,1)}, bf16[192,768]{1,0:T(8,128)(2,1)}, u32[]{:S(2)}, u32[]{:S(2)}) %collective-permute-start.5) | collective-permute-done | bytes 294944 | tf_op jit(solution)/shard_map/ppermute | solution.py:627
  128.0 2.3 collective-permute-start.8
  140.5 2.1 collective-permute-start.14
  147.3 8.7 %first_norm_backward.1 = (f32[1024,768]{1,0:T(8,128)}, bf16[1024,768]{1,0:T(8,128)(2,1)}, f32[8,768]{1,0:T(8,128)}) custom-call(bf16[1024,768]{1,0:T(8,128)(2,1)} %x.5, bf16[1024,768]{1,0:T(8,128)(2,1)} %first_norm_grad.1.part_a, bf16[1024,768]{1,0:T(8,128)(2,1)} %collective-permute-done.11.part_b, f32[2,768]{1,0:T(2,128)} %gains.7, ...), custom_call_target="tpu_custom_call" | custom-call | flops 18874368 | bytes 20971520 | tf_op jit(solution)/shard_map/first_norm_backward/pallas_call | solution.py:575
  160.3 2.1 collective-permute-start.18
  163.8 8.0 %collective-permute-done.18 = bf16[48,1280]{1,0:T(8,128)(2,1)S(1)} collective-permute-done((bf16[48,1280]{1,0:T(8,128)(2,1)S(1)}, bf16[48,1280]{1,0:T(8,128)(2,1)S(1)}, u32[]{:S(2)}, u32[]{:S(2)}) %collective-permute-start.18) | collective-permute-done | bytes 122912 | tf_op jit(solution)/shard_map/ppermute | solution.py:627
  173.6 5.0 %collective-permute-done.21 = bf16[384,768]{1,0:T(8,128)(2,1)S(1)} collective-permute-done((bf16[384,768]{1,0:T(8,128)(2,1)S(1)}, bf16[384,768]{1,0:T(8,128)(2,1)S(1)}, u32[]{:S(2)}, u32[]{:S(2)}) %collective-permute-start.21) | collective-permute-done | bytes 589856 | tf_op jit(solution)/shard_map/ppermute | solution.py:627
  179.3 7.6 %collective-permute-done.25 = bf16[96,1280]{1,0:T(8,128)(2,1)S(1)} collective-permute-done((bf16[96,1280]{1,0:T(8,128)(2,1)S(1)}, bf16[96,1280]{1,0:T(8,128)(2,1)S(1)}, u32[]{:S(2)}, u32[]{:S(2)}) %collective-permute-start.25) | collective-permute-done | bytes 245792 | tf_op jit(solution)/shard_map/ppermute | solution.py:627
  189.8 8.4 %collective-permute-done.26 = bf16[192,1280]{1,0:T(8,128)(2,1)} collective-permute-done((bf16[192,1280]{1,0:T(8,128)(2,1)}, bf16[192,1280]{1,0:T(8,128)(2,1)}, u32[]{:S(2)}, u32[]{:S(2)}) %collective-permute-start.26) | collective-permute-done | bytes 491552 | tf_op jit(solution)/shard_map/ppermute | solution.py:627
  201.0 7.6 %collective-permute-done.27.other = bf16[768,768]{1,0:T(8,128)(2,1)S(1)} collective-permute-done((bf16[768,768]{1,0:T(8,128)(2,1)S(1)}, bf16[768,768]{1,0:T(8,128)(2,1)S(1)}, u32[]{:S(2)}, u32[]{:S(2)}) %collective-permute-start.27) | collective-permute-done | bytes 1179680 | tf_op jit(solution)/shard_map/ppermute | solution.py:627
  208.7 3.1 %join_halves.1 = f32[1536,768]{1,0:T(8,128)} custom-call(s32[1]{0:T(128)} %bitcast.3.half.side, bf16[768,768]{1,0:T(8,128)(2,1)S(1)} %pad_maximum_fusion.1.mine, bf16[768,768]{1,0:T(8,128)(2,1)S(1)} %collective-permute-done.27.other), custom_call_target="tpu_custom_call" | custom-call | bytes 7077888 | tf_op jit(solution)/shard_map/join_halves/pallas_call | solution.py:719
  212.1 2.5 %collective-permute-start.29 = (f32[2,768]{1,0:T(2,128)S(1)}, f32[2,768]{1,0:T(2,128)S(1)}, u32[]{:S(2)}, u32[]{:S(2)}) collective-permute-start(f32[2,768]{1,0:T(2,128)S(1)} %add.244), channel_id=1, source_target_pairs={{0,16},{1,17},{2,18},{3,19},{4,20},{5,21},{6,22},{7,23},{8,24},{9,... | collective-permute-start | bytes 18440 | tf_op jit(solution)/shard_map/ppermute | solution.py:627
  218.1 19.6 %collective-permute-start.32 = (f32[128,768]{0,1:T(8,128)S(1)}, f32[128,768]{0,1:T(8,128)S(1)}, u32[]{:S(2)}, u32[]{:S(2)}) collective-permute-start(f32[128,768]{0,1:T(8,128)S(1)} %bitcast.11), channel_id=1, source_target_pairs={{0,1},{1,0},{2,3},{3,2},{4,5},{5,4},{6,7},{7,6},{8,9},{9,8},{10,11... | collective-permute-start | bytes 1179656 | tf_op jit(solution)/shard_map/ppermute | solution.py:702
  240.0 2.8 %join_up.1 = (f32[768,1536]{1,0:T(8,128)}, f32[384,768]{1,0:T(8,128)}) custom-call(s32[1]{0:T(128)} %bitcast.2.side, bf16[384,1920]{1,0:T(8,128)(2,1)S(1)} %pad_maximum_fusion.mine, bf16[384,1920]{1,0:T(8,128)(2,1)S(1)} %collective-permute-done.31.other), custom_call_target="tpu_custom_call" | custom-call | bytes 8847360 | tf_op jit(solution)/shard_map/join_up/pallas_call | solution.py:753
  (104 shorter events, 46.9 us)
Async XLA Ops:
  48.2 23.1 %collective-permute-start.2 = (bf16[768,768]{1,0:T(8,128)(2,1)}, bf16[768,768]{1,0:T(8,128)(2,1)}, u32[]{:S(2)}, u32[]{:S(2)}) collective-permute-start(bf16[768,768]{1,0:T(8,128)(2,1)} %get-tuple-element.94), channel_id=1, source_target_pairs={{0,2},{1,5},{2,0},{3,7},{4,6},{5,1},{6,4},{7,3},{8,10},{9,13},{10,... | collective-permute-start | bytes 3538952 | tf_op jit(solution)/shard_map/ppermute | solution.py:627
  71.2 32.8 %collective-permute-start.3 = (bf16[384,1920]{1,0:T(8,128)(2,1)}, bf16[384,1920]{1,0:T(8,128)(2,1)}, u32[]{:S(2)}, u32[]{:S(2)}) collective-permute-start(bf16[384,1920]{1,0:T(8,128)(2,1)} %get-tuple-element.101), channel_id=1, source_target_pairs={{0,8},{1,5},{2,10},{3,7},{4,12},{5,1},{6,14},{7,3},{8,0},{9,13},{1... | collective-permute-start | bytes 4423688 | tf_op jit(solution)/shard_map/ppermute | solution.py:627
  72.8 43.1 %collective-permute-start.4 = (bf16[384,768]{1,0:T(8,128)(2,1)S(1)}, bf16[384,768]{1,0:T(8,128)(2,1)S(1)}, u32[]{:S(2)}, u32[]{:S(2)}) collective-permute-start(bf16[384,768]{1,0:T(8,128)(2,1)S(1)} %get-tuple-element.141), channel_id=1, source_target_pairs={{0,4},{1,9},{2,6},{3,11},{4,0},{5,13},{6,2},{7,15},{8,12},{9,1},{1... | collective-permute-start | bytes 1769480 | tf_op jit(solution)/shard_map/ppermute | solution.py:627
  103.9 28.8 %collective-permute-start.7 = (bf16[384,1280]{1,0:T(8,128)(2,1)}, bf16[384,1280]{1,0:T(8,128)(2,1)}, u32[]{:S(2)}, u32[]{:S(2)}) collective-permute-start(bf16[384,1280]{1,0:T(8,128)(2,1)} %get-tuple-element.106), channel_id=1, source_target_pairs={{0,2},{1,9},{2,0},{3,11},{4,6},{5,13},{6,4},{7,15},{8,10},{9,1},{1... | collective-permute-start | bytes 2949128 | tf_op jit(solution)/shard_map/ppermute | solution.py:627
  105.6 24.7 %collective-permute-start.6 = (bf16[192,1920]{1,0:T(8,128)(2,1)S(1)}, bf16[192,1920]{1,0:T(8,128)(2,1)}, u32[]{:S(2)}, u32[]{:S(2)}) collective-permute-start(bf16[192,1920]{1,0:T(8,128)(2,1)S(1)} %get-tuple-element.139), channel_id=1, source_target_pairs={{0,2},{1,9},{2,0},{3,11},{4,6},{5,13},{6,4},{7,15},{8,10},{9,1},{1... | collective-permute-start | bytes 2211848 | tf_op jit(solution)/shard_map/ppermute | solution.py:627
  113.5 32.6 %collective-permute-start.12 = (bf16[1024,768]{1,0:T(8,128)(2,1)}, bf16[1024,768]{1,0:T(8,128)(2,1)S(1)}, u32[]{:S(2)}, u32[]{:S(2)}) collective-permute-start(bf16[1024,768]{1,0:T(8,128)(2,1)} %down_projection.1.fold_a), channel_id=1, source_target_pairs={{0,1},{1,0},{2,3},{3,2},{4,5},{5,4},{6,7},{7,6},{8,9},{9,8},{10,11... | collective-permute-start | bytes 4718600 | tf_op jit(solution)/shard_map/ppermute | solution.py:702
  116.8 9.4 %collective-permute-start.5 = (bf16[192,768]{1,0:T(8,128)(2,1)}, bf16[192,768]{1,0:T(8,128)(2,1)}, u32[]{:S(2)}, u32[]{:S(2)}) collective-permute-start(bf16[192,768]{1,0:T(8,128)(2,1)} %get-tuple-element.151), channel_id=1, source_target_pairs={{0,8},{1,3},{2,10},{3,1},{4,12},{5,7},{6,14},{7,5},{8,0},{9,11},{1... | collective-permute-start | bytes 884744 | tf_op jit(solution)/shard_map/ppermute | solution.py:627
  123.5 22.6 %collective-permute-start.11 = (bf16[1024,768]{1,0:T(8,128)(2,1)}, bf16[1024,768]{1,0:T(8,128)(2,1)}, u32[]{:S(2)}, u32[]{:S(2)}) collective-permute-start(bf16[1024,768]{1,0:T(8,128)(2,1)} %first_norm_grad.1.part_a), channel_id=1, source_target_pairs={{0,1},{1,0},{2,3},{3,2},{4,5},{5,4},{6,7},{7,6},{8,9},{9,8},{10,11... | collective-permute-start | bytes 4718600 | tf_op jit(solution)/shard_map/ppermute | solution.py:702
  128.0 10.0 %collective-permute-start.8 = (bf16[96,768]{1,0:T(8,128)(2,1)}, bf16[96,768]{1,0:T(8,128)(2,1)}, u32[]{:S(2)}, u32[]{:S(2)}) collective-permute-start(bf16[96,768]{1,0:T(8,128)(2,1)} %get-tuple-element.163), channel_id=1, source_target_pairs={{0,16},{1,17},{2,18},{3,19},{4,20},{5,21},{6,22},{7,23},{8,24},{9,... | collective-permute-start | bytes 442376 | tf_op jit(solution)/shard_map/ppermute | solution.py:627
  134.1 10.5 %collective-permute-start.10 = (bf16[192,1280]{1,0:T(8,128)(2,1)S(1)}, bf16[192,1280]{1,0:T(8,128)(2,1)}, u32[]{:S(2)}, u32[]{:S(2)}) collective-permute-start(bf16[192,1280]{1,0:T(8,128)(2,1)S(1)} %get-tuple-element.143), channel_id=1, source_target_pairs={{0,4},{1,3},{2,6},{3,1},{4,0},{5,7},{6,2},{7,5},{8,12},{9,11},{10,... | collective-permute-start | bytes 1474568 | tf_op jit(solution)/shard_map/ppermute | solution.py:627
  139.0 16.9 %collective-permute-start.13 = (bf16[96,768]{1,0:T(8,128)(2,1)S(1)}, bf16[96,768]{1,0:T(8,128)(2,1)S(1)}, u32[]{:S(2)}, u32[]{:S(2)}) collective-permute-start(bf16[96,768]{1,0:T(8,128)(2,1)S(1)} %add_convert_fusion.15), channel_id=1, source_target_pairs={{0,16},{1,17},{2,18},{3,19},{4,20},{5,21},{6,22},{7,23},{8,24},{9,... | collective-permute-start | bytes 442376 | tf_op jit(solution)/shard_map/ppermute | solution.py:627
  140.5 17.9 %collective-permute-start.14 = (bf16[48,1920]{1,0:T(8,128)(2,1)S(1)}, bf16[48,1920]{1,0:T(8,128)(2,1)S(1)}, u32[]{:S(2)}, u32[]{:S(2)}) collective-permute-start(bf16[48,1920]{1,0:T(8,128)(2,1)S(1)} %get-tuple-element.159), channel_id=1, source_target_pairs={{0,16},{1,17},{2,18},{3,19},{4,20},{5,21},{6,22},{7,23},{8,24},{9,... | collective-permute-start | bytes 552968 | tf_op jit(solution)/shard_map/ppermute | solution.py:627
  145.8 14.4 %collective-permute-start.16 = (bf16[96,1280]{1,0:T(8,128)(2,1)S(1)}, bf16[96,1280]{1,0:T(8,128)(2,1)S(1)}, u32[]{:S(2)}, u32[]{:S(2)}) collective-permute-start(bf16[96,1280]{1,0:T(8,128)(2,1)S(1)} %get-tuple-element.155), channel_id=1, source_target_pairs={{0,8},{1,5},{2,10},{3,7},{4,12},{5,1},{6,14},{7,3},{8,0},{9,13},{1... | collective-permute-start | bytes 737288 | tf_op jit(solution)/shard_map/ppermute | solution.py:627
  158.5 13.4 %collective-permute-start.19 = (bf16[48,1920]{1,0:T(8,128)(2,1)S(1)}, bf16[48,1920]{1,0:T(8,128)(2,1)S(1)}, u32[]{:S(2)}, u32[]{:S(2)}) collective-permute-start(bf16[48,1920]{1,0:T(8,128)(2,1)S(1)} %add_convert_fusion.12), channel_id=1, source_target_pairs={{0,16},{1,17},{2,18},{3,19},{4,20},{5,21},{6,22},{7,23},{8,24},{9,... | collective-permute-start | bytes 552968 | tf_op jit(solution)/shard_map/ppermute | solution.py:627
  159.9 13.4 %collective-permute-start.20 = (f32[2,768]{1,0:T(2,128)S(1)}, f32[2,768]{1,0:T(2,128)S(1)}, u32[]{:S(2)}, u32[]{:S(2)}) collective-permute-start(f32[2,768]{1,0:T(2,128)S(1)} %add.239), channel_id=1, source_target_pairs={{0,4},{1,9},{2,6},{3,11},{4,0},{5,13},{6,2},{7,15},{8,12},{9,1},{1... | collective-permute-start | bytes 18440 | tf_op jit(solution)/shard_map/ppermute | solution.py:627
  160.3 11.5 %collective-permute-start.18 = (bf16[48,1280]{1,0:T(8,128)(2,1)S(1)}, bf16[48,1280]{1,0:T(8,128)(2,1)S(1)}, u32[]{:S(2)}, u32[]{:S(2)}) collective-permute-start(bf16[48,1280]{1,0:T(8,128)(2,1)S(1)} %get-tuple-element.167), channel_id=1, source_target_pairs={{0,16},{1,17},{2,18},{3,19},{4,20},{5,21},{6,22},{7,23},{8,24},{9,... | collective-permute-start | bytes 368648 | tf_op jit(solution)/shard_map/ppermute | solution.py:627
  162.5 16.1 %collective-permute-start.21 = (bf16[384,768]{1,0:T(8,128)(2,1)S(1)}, bf16[384,768]{1,0:T(8,128)(2,1)S(1)}, u32[]{:S(2)}, u32[]{:S(2)}) collective-permute-start(bf16[384,768]{1,0:T(8,128)(2,1)S(1)} %pad_maximum_fusion.4), channel_id=1, source_target_pairs={{0,4},{1,9},{2,6},{3,11},{4,0},{5,13},{6,2},{7,15},{8,12},{9,1},{1... | collective-permute-start | bytes 1769480 | tf_op jit(solution)/shard_map/ppermute | solution.py:627
  178.9 8.0 %collective-permute-start.25 = (bf16[96,1280]{1,0:T(8,128)(2,1)S(1)}, bf16[96,1280]{1,0:T(8,128)(2,1)S(1)}, u32[]{:S(2)}, u32[]{:S(2)}) collective-permute-start(bf16[96,1280]{1,0:T(8,128)(2,1)S(1)} %pad_maximum_fusion.8), channel_id=1, source_target_pairs={{0,8},{1,5},{2,10},{3,7},{4,12},{5,1},{6,14},{7,3},{8,0},{9,13},{1... | collective-permute-start | bytes 737288 | tf_op jit(solution)/shard_map/ppermute | solution.py:627
  187.7 10.4 %collective-permute-start.26 = (bf16[192,1280]{1,0:T(8,128)(2,1)}, bf16[192,1280]{1,0:T(8,128)(2,1)}, u32[]{:S(2)}, u32[]{:S(2)}) collective-permute-start(bf16[192,1280]{1,0:T(8,128)(2,1)} %pad_maximum_fusion.5), channel_id=1, source_target_pairs={{0,4},{1,3},{2,6},{3,1},{4,0},{5,7},{6,2},{7,5},{8,12},{9,11},{10,... | collective-permute-start | bytes 1474568 | tf_op jit(solution)/shard_map/ppermute | solution.py:627
  188.0 20.6 %collective-permute-start.27 = (bf16[768,768]{1,0:T(8,128)(2,1)S(1)}, bf16[768,768]{1,0:T(8,128)(2,1)S(1)}, u32[]{:S(2)}, u32[]{:S(2)}) collective-permute-start(bf16[768,768]{1,0:T(8,128)(2,1)S(1)} %pad_maximum_fusion.1.mine), channel_id=1, source_target_pairs={{0,2},{1,5},{2,0},{3,7},{4,6},{5,1},{6,4},{7,3},{8,10},{9,13},{10,... | collective-permute-start | bytes 3538952 | tf_op jit(solution)/shard_map/ppermute | solution.py:627
  188.0 23.7 %collective-permute-start.28 = (bf16[192,1920]{1,0:T(8,128)(2,1)S(1)}, bf16[192,1920]{1,0:T(8,128)(2,1)S(1)}, u32[]{:S(2)}, u32[]{:S(2)}) collective-permute-start(bf16[192,1920]{1,0:T(8,128)(2,1)S(1)} %pad_maximum_fusion.3), channel_id=1, source_target_pairs={{0,2},{1,9},{2,0},{3,11},{4,6},{5,13},{6,4},{7,15},{8,10},{9,1},{1... | collective-permute-start | bytes 2211848 | tf_op jit(solution)/shard_map/ppermute | solution.py:627
  199.5 16.7 %collective-permute-start.30 = (bf16[384,1280]{1,0:T(8,128)(2,1)S(1)}, bf16[384,1280]{1,0:T(8,128)(2,1)S(1)}, u32[]{:S(2)}, u32[]{:S(2)}) collective-permute-start(bf16[384,1280]{1,0:T(8,128)(2,1)S(1)} %pad_maximum_fusion.2.mine), channel_id=1, source_target_pairs={{0,2},{1,9},{2,0},{3,11},{4,6},{5,13},{6,4},{7,15},{8,10},{9,1},{1... | collective-permute-start | bytes 2949128 | tf_op jit(solution)/shard_map/ppermute | solution.py:627
  212.0 28.0 %collective-permute-start.31 = (bf16[384,1920]{1,0:T(8,128)(2,1)S(1)}, bf16[384,1920]{1,0:T(8,128)(2,1)S(1)}, u32[]{:S(2)}, u32[]{:S(2)}) collective-permute-start(bf16[384,1920]{1,0:T(8,128)(2,1)S(1)} %pad_maximum_fusion.mine), channel_id=1, source_target_pairs={{0,8},{1,5},{2,10},{3,7},{4,12},{5,1},{6,14},{7,3},{8,0},{9,13},{1... | collective-permute-start | bytes 4423688 | tf_op jit(solution)/shard_map/ppermute | solution.py:627
  218.1 21.0 %collective-permute-start.32 = (f32[128,768]{0,1:T(8,128)S(1)}, f32[128,768]{0,1:T(8,128)S(1)}, u32[]{:S(2)}, u32[]{:S(2)}) collective-permute-start(f32[128,768]{0,1:T(8,128)S(1)} %bitcast.11), channel_id=1, source_target_pairs={{0,1},{1,0},{2,3},{3,2},{4,5},{5,4},{6,7},{7,6},{8,9},{9,8},{10,11... | collective-permute-start | bytes 1179656 | tf_op jit(solution)/shard_map/ppermute | solution.py:702
  (15 other events, 104.9 us)
where the time goes:
time: 245 us; the launch traced here: 243 us
  Pallas kernels  120 us (49%)
  starting transfers between devices  49.9 us (20%)
  waiting for transfers between devices  49.3 us (20%)
  other arithmetic  16.3 us (7%)
  local copies, waits for them, and re-layouts  5.91 us (2%)
    ppermute x28, waiting for transfers between devices, swap(): return lax.ppermute(value, ('dp', 'tensor'), pairs)  44.4 us
    pallas_call x1, Pallas kernels, backward(): pl.pallas_call(functools.partial(backward_kernel, n, heads), grid=(n,), i...  29.5 us
    ppermute x28, starting transfers between devices, swap(): return lax.ppermute(value, ('dp', 'tensor'), pairs)  27.3 us
    pallas_call x1, Pallas kernels, forward(): pl.pallas_call(functools.partial(forward_kernel, heads), grid=(n,), in_sp...  25.5 us
    ppermute x5, starting transfers between devices, swap_tensor(): return lax.ppermute(value, 'tensor', [(t, t ^ 1) for t in range(n_tensor)])  22.6 us
    pallas_call x1, Pallas kernels, feed(): pl.pallas_call(feed_kernel, grid=(t // BLK,), in_specs=[smem(), rows(d),...  17.1 us
    pallas_call x1, Pallas kernels, middle(): pl.pallas_call(functools.partial(middle_kernel, hd), grid=(t // BLK,), in...  14.3 us
    convert_element_type x9, other arithmetic, cut(): return (pieces[0].astype(F32) + pieces[1].astype(F32)).astype(BF)  11.7 us
  transfers between devices with their start and end apart: 33, of which 12 were waited for; matrix products, arithmetic and copies ran while one was open for 7% of the time, Pallas kernels for 31%

commit v1 on v0

--- a/solution.py
+++ b/solution.py
@@ -21,8 +21,10 @@
 UP = (2, 0, 1, 3), (1, 2, 0, 3)
 ATT = (0, 1, 2, 3), (2, 0, 1, 3)
 EARLY = "d"
-LATE = "udnduabduafdugadaugdaugaddaaDuugggAU"
-FREE = True
+LATE = "dbudnudaufuadaudaugaddugaagdDagAgguU"
+FREE = False
+
+SHARES = (3.0, 3.0, 3.0, 3.0, 3.0, 3.0)
 
 
 def mm(a, b):
@@ -43,9 +45,10 @@
     )
 
 
-def cost(flops, nbytes, trans=0):
+def cost(flops, nbytes, trans=0, share=1.0):
     return pl.CostEstimate(
-        flops=int(COST * flops), bytes_accessed=int(COST * nbytes), transcendentals=int(COST * trans)
+        flops=int(COST * share * flops), bytes_accessed=int(COST * share * nbytes),
+        transcendentals=int(COST * share * trans),
     )
 
 
@@ -59,6 +62,21 @@
 
 def rows(width, count=BLK):
     return pl.BlockSpec((count, width), lambda i, *_: (i, 0))
+
+
+def anywhere():
+    return pl.BlockSpec(memory_space=pl.ANY)
+
+
+def fetch(start, wait, *copies):
+    for condition, act in ((start, "start"), (wait, "wait")):
+        if condition is None:
+            continue
+
+        @pl.when(condition)
+        def _():
+            for copy in copies:
+                getattr(pltpu.make_async_copy(*copy), act)()
 
 
 def smem():
@@ -115,7 +133,6 @@
     def _():
         carry_s[...] = jnp.zeros_like(carry_s)
         qx_s[...] = jnp.zeros_like(qx_s)
-        sk_s[...] = jnp.zeros_like(sk_s)
         seg, first = sequence_ids(lens, lax.broadcasted_iota(jnp.int32, (t, 1), 0))
         seg_s[:, 0:1] = seg
         seg_s[:, 1:2] = jnp.where(first, -1, seg)
@@ -146,35 +163,38 @@
             ]
 
     row = step * BLK + lax.broadcasted_iota(jnp.int32, (1, BLK), 1)
-    col = lax.broadcasted_iota(jnp.int32, (t, 1), 0)
     seg_i, _ = sequence_ids(lens, row)
-    sel = jnp.maximum(mm_nt(sk_s[...], sq), 0.0)
-    picked = jnp.where((seg_s[:, 1:2] == seg_i) & (col < row), sel * sel, 0.0)
-    pen = split_dot(picked, triangle(False)) + carry_s[:, 0:1]
-    carry_s[:, 0:1] = pen[:, BLK - 1 : BLK] + picked[:, BLK - 1 : BLK]
-    pen_o[...] = jnp.where((seg_s[:, 0:1] == seg_i) & (col <= row), pen, NOT_ATTENDED)
-
+    before = triangle(False)
     top_s[...] = jnp.full_like(top_s, -NOT_ATTENDED)
     sum_s[...] = jnp.zeros_like(sum_s)
     acc_s[...] = jnp.zeros_like(acc_s)
 
     def tile(j, _):
         at = rows_of(j)
-        bias = pen_o[at, :]
+        raw = [mm(k_s[at, p * two : (p + 1) * two], qx_s[p]) for p in range(pairs)]
+        col = j * BLK + lax.broadcasted_iota(jnp.int32, (BLK, 1), 0)
+        sel = jnp.maximum(mm_nt(sk_s[at, :], sq), 0.0)
+        picked = jnp.where((seg_s[at, 1:2] == seg_i) & (col < row), sel * sel, 0.0)
+        pen = split_dot(picked, before) + carry_s[at, 0:1]
+        carry_s[at, 0:1] = pen[:, BLK - 1 : BLK] + picked[:, BLK - 1 : BLK]
+        bias = jnp.where((seg_s[at, 0:1] == seg_i) & (col <= row), pen, NOT_ATTENDED)
+        pen_o[at, :] = bias
         bias = jnp.concatenate([bias, bias], axis=1)
+        lows, fades = [], []
         for p in range(pairs):
-            s = mm(k_s[at, p * two : (p + 1) * two], qx_s[p]) - bias
+            s = raw[p] - bias
             old = top_s[p : p + 1, :]
             top = jnp.maximum(old, jnp.max(s, axis=0, keepdims=True))
             fade = jnp.exp(old - top)
             prob = jnp.exp(s - top)
             top_s[p : p + 1, :] = top
             sum_s[p : p + 1, :] = sum_s[p : p + 1, :] * fade + jnp.sum(prob, axis=0, keepdims=True)
-            low = prob.astype(BF)
-            for side in range(2):
-                mine = slice((2 * p + side) * hd, (2 * p + side + 1) * hd)
-                cut = slice(side * BLK, (side + 1) * BLK)
-                acc_s[mine, :] = acc_s[mine, :] * fade[:, cut] + mm(vt_s[mine, at], low[:, cut])
+            lows.append(prob.astype(BF))
+            fades.append(fade)
+        for h in range(heads):
+            p, cut = h // 2, slice((h % 2) * BLK, (h % 2 + 1) * BLK)
+            mine = slice(h * hd, (h + 1) * hd)
+            acc_s[mine, :] = acc_s[mine, :] * fades[p][:, cut] + mm(vt_s[mine, at], lows[p][:, cut])
         return 0
 
     lax.fori_loop(0, step + 1, tile, 0)
@@ -234,12 +254,12 @@
     h2 = (mid * norm_scale(mid) * gains[1:2, :]).astype(BF)
     h2_o[...] = h2
     hidden = up.shape[1]
-    chunk = 512
-    dn = jnp.zeros(mid.shape, F32)
-    for c in range(hidden // chunk):
-        cut = slice(c * chunk, (c + 1) * chunk)
-        u = mm(h2, up[:, cut])
-        da = mm_nt(g[here, :], down[cut, :])
+    chunk = hidden
+    cuts = [slice(c, c + chunk) for c in range(0, hidden, chunk)]
+    ups = [mm(h2, up[:, cut]) for cut in cuts]
+    das = [mm_nt(g[here, :], down[cut, :]) for cut in cuts]
+    dus = []
+    for u, da, cut in zip(ups, das, cuts):
         u2 = u * u
         curve = jnp.tanh(u * (CURVE + (CURVE * CUBE) * u2))
         part = 0.5 * (1.0 + curve)
@@ -249,15 +269,15 @@
         act_o[:, cut] = act
         act_s[here, cut] = act
         du_o[:, cut] = du
-        dn = dn + mm_nt(du, up[:, cut])
+        dus.append(du)
+    dn = functools.reduce(jnp.add, [mm_nt(du, up[:, cut]) for du, cut in zip(dus, cuts)])
     dn_o[...] = dn.astype(BF)
 
     @pl.when(step == pl.num_programs(0) - 1)
     def _():
-        tile = 128
-        for j in range(dsend_o.shape[0] // tile):
-            at = pl.ds(pl.multiple_of(half[0] * dsend_o.shape[0] + j * tile, tile), tile)
-            dsend_o[j * tile : (j + 1) * tile, :] = mm_tn(act_s[:, at], g[...]).astype(BF)
+        size = dsend_o.shape[0]
+        at = pl.ds(pl.multiple_of(half[0] * size, 128), size)
+        dsend_o[...] = mm_tn(act_s[:, at], g[...]).astype(BF)
 
 
 def feed(half, x, part_a, part_b, gains, up, down, g):
@@ -319,22 +339,27 @@
 
 
 def middle_kernel(
-    hd, half, mid, part_a, part_b, gains, g, wout, mixed, h2, du, dmid_o, gm_o, dmix_o, dots_o,
-    send_o, keep_o, gain_o, gm_s,
+    hd, half, mid, part_a, part_b, gains, g, wout, mixed_row, mixed_in, h2_in, du_in, dmid_o,
+    dmix_o, dots_o, send_o, keep_o, gain_o, gm_s, mixed, h2, du, sems,
 ):
     step = pl.program_id(0)
     here = rows_of(step)
+    final = step == pl.num_programs(0) - 1
+    late = [
+        (source, target, sems.at[n])
+        for n, (source, target) in enumerate(((h2_in, h2), (du_in, du), (mixed_in, mixed)))
+    ]
+    fetch(step == 0, None, *late)
     values = mid[...]
     grad = part_a[...].astype(F32) + part_b[...].astype(F32)
     back, gain_grad = norm_back(values, norm_scale(values), gains[1:2, :], grad)
     dmid = g[...].astype(F32) + back
     dmid_o[...] = dmid
     gm = dmid.astype(BF)
-    gm_o[...] = gm
     gm_s[here, :] = gm
     dmix = mm_nt(gm, wout[...]).astype(BF)
     dmix_o[...] = dmix
-    both = (dmix.astype(F32) * mixed[here, :].astype(F32)).T
+    both = (dmix.astype(F32) * mixed_row[...].astype(F32)).T
     for h in range(both.shape[0] // hd):
         dots_o[h : h + 1, :] = jnp.sum(both[h * hd : (h + 1) * hd, :], axis=0, keepdims=True)
 
@@ -343,19 +368,16 @@
         gain_o[...] = jnp.zeros_like(gain_o)
 
     gain_o[0:1, :] += gain_grad
-
-    @pl.when(step == pl.num_programs(0) - 1)
+    fetch(None, final, *late)
+
+    @pl.when(final)
     def _():
         hidden = du.shape[1]
         size = send_o.shape[0]
-        tile = 128
         for which, into in ((half[0], send_o), (1 - half[0], keep_o)):
-            half_at = pl.multiple_of(which * size, tile)
-            for r in range(size // tile):
-                out = slice(r * tile, (r + 1) * tile)
-                at = pl.ds(pl.multiple_of(half_at + r * tile, tile), tile)
-                into[out, :hidden] = mm_tn(h2[:, at], du[...]).astype(BF)
-                into[out, hidden:] = mm_tn(mixed[:, out], gm_s[:, pl.ds(half_at, size)]).astype(BF)
+            at = pl.ds(pl.multiple_of(which * size, 128), size)
+            into[:, :hidden] = mm_tn(h2[:, at], du[...]).astype(BF)
+            into[:, hidden:] = mm_tn(mixed[...], gm_s[:, at]).astype(BF)
 
 
 def middle(half, mid, part_a, part_b, gains, g, wout, mixed, h2, du, hd):
@@ -367,22 +389,25 @@
         grid=(t // BLK,),
         in_specs=[
             smem(), rows(d), rows(d), rows(d), whole(*gains.shape), rows(d), whole(*wout.shape),
-            whole(t, wh), whole(t, d), whole(t, hidden),
+            rows(wh), anywhere(), anywhere(), anywhere(),
         ],
         out_specs=[
-            rows(d), rows(d), rows(wh), pl.BlockSpec((8, BLK), lambda i: (0, i)),
+            rows(d), rows(wh), pl.BlockSpec((8, BLK), lambda i: (0, i)),
             whole(d // 2, hidden + d // 2), whole(d // 2, hidden + d // 2), whole(8, d),
         ],
         out_shape=[
-            shape((t, d), F32), shape((t, d), BF), shape((t, wh), BF), shape((8, t), F32),
+            shape((t, d), F32), shape((t, wh), BF), shape((8, t), F32),
             shape((d // 2, hidden + d // 2), BF), shape((d // 2, hidden + d // 2), BF),
             shape((8, d), F32),
         ],
-        scratch_shapes=[pltpu.VMEM((t, d), BF)],
+        scratch_shapes=[
+            pltpu.VMEM((t, d), BF), pltpu.VMEM((t, wh), BF), pltpu.VMEM((t, d), BF),
+            pltpu.VMEM((t, hidden), BF), pltpu.SemaphoreType.DMA((3,)),
+        ],
         compiler_params=params(),
         cost_estimate=cost(2 * t * d * wh + t * d * hidden, 20 * MIB),
         name="second_norm_backward",
-    )(half, mid, part_a, part_b, gains, g, wout, mixed, h2, du)
+    )(half, mid, part_a, part_b, gains, g, wout, mixed, mixed, h2, du)
 
 
 def split_three(values):
@@ -393,10 +418,12 @@
 
 
 def backward_kernel(
-    n_blocks, heads, lens, half, q, k, v, sq, sk, pen, lse, dots, dmix, h1, cat_o, send_o, keep_o,
-    qx_s, qm_s, dx_s, dm_s, dq_s, dsq_s, dk_s, dv_s, dsk_s, kt_s, skt_s, kx_s, vx_s, seg_s,
+    n_blocks, heads, lens, half, q, k, v, sq, sk, pen, lse, dots, dmix, h1_in, cat_o, send_o, keep_o,
+    qx_s, qm_s, dx_s, dm_s, dq_s, dsq_s, dk_s, dv_s, dsk_s, kt_s, skt_s, kx_s, vx_s, seg_s, h1, sems,
 ):
     j = pl.program_id(0)
+    late = (h1_in, h1, sems.at[0])
+    fetch(j == 0, None, late)
     wh = k.shape[1]
     hd = sk.shape[1]
     t = q.shape[0]
@@ -456,25 +483,31 @@
         i = n_blocks - 1 - back
         at = rows_of(i)
         bias = pen[:, at]
+        bias = jnp.concatenate([bias, bias], axis=1)
+        scores = [mm(kx_s[p], qx_s[p, i]) - bias for p in range(pairs)]
+        dprobs = [mm(vx_s[p], dx_s[p, i]) for p in range(pairs)]
+        sel = jnp.maximum(mm_nt(sk[...], sq[at, :]), 0.0)
         dpen = None
+        probs, lows = [], []
+        for p in range(pairs):
+            prob = jnp.exp(scores[p])
+            dscore = prob * dprobs[p]
+            both = dscore[:, :BLK] + dscore[:, BLK:]
+            dpen = both if dpen is None else dpen + both
+            probs.append(prob.astype(BF))
+            lows.append(dscore.astype(BF))
         for p in range(pairs):
             pair = slice(p * two, (p + 1) * two)
-            prob = jnp.exp(mm(kx_s[p], qx_s[p, i]) - jnp.concatenate([bias, bias], axis=1))
-            dscore = prob * mm(vx_s[p], dx_s[p, i])
-            both = dscore[:, :BLK] + dscore[:, BLK:]
-            dpen = both if dpen is None else dpen + both
-            low = dscore.astype(BF)
             for side in range(2):
                 h = 2 * p + side
                 dq_s[p, side * hd : (side + 1) * hd, at] += mm(
-                    kt_s[h * hd : (h + 1) * hd, :], low[:, side * BLK : (side + 1) * BLK]
+                    kt_s[h * hd : (h + 1) * hd, :], lows[p][:, side * BLK : (side + 1) * BLK]
                 )
-            dv_s[:, pair] += mm(prob.astype(BF), dm_s[p, i])
-            dk_s[:, pair] += mm(low, qm_s[p, i])
+            dv_s[:, pair] += mm(probs[p], dm_s[p, i])
+            dk_s[:, pair] += mm(lows[p], qm_s[p, i])
         dpicked = split_dot(dpen, after) + carry
         row = i * BLK + lax.broadcasted_iota(jnp.int32, (1, BLK), 1)
         chosen = (seg_j == seg_s[0:1, at]) & (col < row)
-        sel = jnp.maximum(mm_nt(sk[...], sq[at, :]), 0.0)
         dsel = jnp.where(chosen, -2.0 * dpicked * sel, 0.0).astype(BF)
         dsk_s[...] += mm(dsel, sq[at, :])
         dsq_s[:, at] += mm(skt_s[...], dsel)
@@ -484,6 +517,8 @@
     cat_o[here, wh : 2 * wh] = dk_s[...].astype(BF)
     cat_o[here, 2 * wh : 3 * wh] = dv_s[...].astype(BF)
     cat_o[here, 3 * wh + hd : 3 * wh + 2 * hd] = dsk_s[...].astype(BF)
+
+    fetch(None, j == n_blocks - 1, late)
 
     @pl.when(j == n_blocks - 1)
     def _():
@@ -491,11 +526,9 @@
             cat_o[:, p * two : (p + 1) * two] = (dq_s[p] * scale).T.astype(BF)
         cat_o[:, 3 * wh : 3 * wh + hd] = (dsq_s[...] * scale).T.astype(BF)
         size = send_o.shape[0]
-        tile = 128
         for which, into in ((half[0], send_o), (1 - half[0], keep_o)):
-            for r in range(size // tile):
-                at = pl.ds(pl.multiple_of(which * size + r * tile, tile), tile)
-                into[r * tile : (r + 1) * tile, :] = mm_tn(h1[:, at], cat_o[...]).astype(BF)
+            at = pl.ds(pl.multiple_of(which * size, 128), size)
+            into[...] = mm_tn(h1[:, at], cat_o[...]).astype(BF)
 
 
 def backward(lens, half, q, k, v, sq, sk, pen, lse, dots, dmix, h1):
@@ -512,7 +545,7 @@
         grid=(n,),
         in_specs=[
             smem(), smem(), whole(t, wh), rows(wh), rows(wh), whole(t, hd), rows(hd), rows(t),
-            whole(8, t), whole(8, t), whole(t, wh), whole(t, d),
+            whole(8, t), whole(8, t), whole(t, wh), anywhere(),
         ],
         out_specs=[whole(t, width), whole(d // 2, width), whole(d // 2, width)],
         out_shape=[
@@ -524,6 +557,7 @@
             pltpu.VMEM((BLK, wh), F32), pltpu.VMEM((BLK, hd), F32), pltpu.VMEM((wh, BLK), BF),
             pltpu.VMEM((hd, BLK), BF), pltpu.VMEM((heads // 2, BLK, 4 * hd), BF),
             pltpu.VMEM((heads // 2, BLK, 4 * hd), BF), pltpu.VMEM((8, t), jnp.int32),
+            pltpu.VMEM((t, d), BF), pltpu.SemaphoreType.DMA((1,)),
         ],
         compiler_params=params(),
         cost_estimate=cost(10 * heads * t * t * hd, 12 * MIB, heads * t * t),
@@ -549,7 +583,7 @@
         out_specs=rows(d),
         out_shape=shape((t, d), BF),
         compiler_params=params(),
-        cost_estimate=cost(2 * t * d * width, 6 * MIB),
+        cost_estimate=cost(2 * t * d * width, 6 * MIB, share=SHARES[0]),
         name="first_norm_grad",
     )(cat, wqkv, wsel)
 
@@ -579,7 +613,7 @@
         out_specs=[rows(d), rows(d), whole(8, d)],
         out_shape=[shape((t, d), F32), shape((t, d), BF), shape((8, d), F32)],
         compiler_params=params(),
-        cost_estimate=cost(24 * t * d, 20 * MIB),
+        cost_estimate=cost(24 * t * d, 20 * MIB, share=SHARES[2]),
         name="first_norm_backward",
     )(x, part_a, part_b, gains, dmid, mid, fold_a, fold_b)
 
@@ -598,7 +632,7 @@
         out_specs=rows(d),
         out_shape=shape((t, d), BF),
         compiler_params=params(),
-        cost_estimate=cost(2 * t * d * hidden, 8 * MIB),
+        cost_estimate=cost(2 * t * d * hidden, 8 * MIB, share=SHARES[1]),
         name="down_projection",
     )(act, down)
 
@@ -733,7 +767,7 @@
         compiler_params=pltpu.CompilerParams(
             dimension_semantics=("arbitrary", "arbitrary"), vmem_limit_bytes=32 * MIB
         ),
-        cost_estimate=cost(0, 12 * r * n),
+        cost_estimate=cost(0, 12 * r * n, share=SHARES[3]),
         name="join_halves",
     )(side, mine, other)
 
@@ -763,7 +797,7 @@
         ),
         out_shape=[shape((2 * r, hidden), F32), shape((wh, 2 * r), F32)],
         compiler_params=params(32),
-        cost_estimate=cost(0, 12 * r * n),
+        cost_estimate=cost(0, 12 * r * n, share=SHARES[4]),
         name="join_up",
     )(side, mine, other)
 
@@ -794,7 +828,7 @@
         ),
         out_shape=[shape((3, 2 * r, wh), F32), shape((2 * r, 2 * hd), F32)],
         compiler_params=params(32),
-        cost_estimate=cost(0, 12 * r * n),
+        cost_estimate=cost(0, 12 * r * n, share=SHARES[5]),
         name="join_attention",
     )(side, mine, other)
 
@@ -828,7 +862,7 @@
     dn2_other = swap(dn2)
     down.begin(down_send)
     down.hold(*run(lambda act, *v: [down_half(down_kept, act, *v)], act, grad_output))
-    dmid, gm, dmix, dots, up_send, up_keep, gain_two = run(
+    dmid, dmix, dots, up_send, up_keep, gain_two = run(
         lambda dn2, *v: middle(1 - up_kept, mid, dn2, *v, hd),
         dn2, dn2_other, norm_gains, grad_output, out_weight, mixed, h2, du,
     )

time: 245 us -> 221 us (0.902)
  starting transfers between devices: 49.9 us -> 31 us
  waiting for transfers between devices: 49.3 us -> 60.4 us
  other arithmetic: 16.3 us -> 9.26 us
  Pallas kernels: 120 us -> 113 us
    ppermute x5, starting transfers between devices: 22.6 us -> 3.25 us  [swap_tensor(): return lax.ppermute(value, 'tensor', [(t, t ^ 1) for t in range(n_tensor)])]
    ppermute x28, waiting for transfers between devices: 44.4 us -> 56.8 us  [swap(): return lax.ppermute(value, ('dp', 'tensor'), pairs)]
    convert_element_type x9, other arithmetic: 11.7 us -> 7.48 us  [cut(): return (pieces[0].astype(F32) + pieces[1].astype(F32)).astype(BF)]
    pallas_call x1, Pallas kernels: 29.5 us -> 26 us  [backward(): pl.pallas_call(functools.partial(backward_kernel, n, heads), grid=(n,), i...]
    pallas_call x1, Pallas kernels: 25.5 us -> 22.6 us  [forward(): pl.pallas_call(functools.partial(forward_kernel, heads), grid=(n,), in_sp...]
  transfers between devices with their start and end apart: 33 -> 33, of which waited for: 12 -> 16; matrix products, arithmetic and copies ran while one was open for 7% -> 5% of each run, Pallas kernels for 31% -> 33%
where the time goes in v1:
time: 221 us; the launch traced here: 220 us
  Pallas kernels  113 us (51%)
  waiting for transfers between devices  60.4 us (27%)
  starting transfers between devices  31 us (14%)
  other arithmetic  9.26 us (4%)
  local copies, waits for them, and re-layouts  5.91 us (3%)
    ppermute x28, waiting for transfers between devices, swap(): return lax.ppermute(value, ('dp', 'tensor'), pairs)  56.8 us
    ppermute x28, starting transfers between devices, swap(): return lax.ppermute(value, ('dp', 'tensor'), pairs)  27.7 us
    pallas_call x1, Pallas kernels, backward(): pl.pallas_call(functools.partial(backward_kernel, n, heads), grid=(n,), i...  26 us
    pallas_call x1, Pallas kernels, forward(): pl.pallas_call(functools.partial(forward_kernel, heads), grid=(n,), in_sp...  22.6 us
    pallas_call x1, Pallas kernels, feed(): pl.pallas_call(feed_kernel, grid=(t // BLK,), in_specs=[smem(), rows(d),...  16.8 us
    pallas_call x1, Pallas kernels, middle(): pl.pallas_call(functools.partial(middle_kernel, hd), grid=(t // BLK,), in...  13.2 us
    pallas_call x1, Pallas kernels, finish(): pl.pallas_call(finish_kernel, grid=(t // BLK,), in_specs=[rows(d), rows(d...  8.81 us
    convert_element_type x9, other arithmetic, cut(): return (pieces[0].astype(F32) + pieces[1].astype(F32)).astype(BF)  7.48 us
  transfers between devices with their start and end apart: 33, of which 16 were waited for; matrix products, arithmetic and copies ran while one was open for 5% of the time, Pallas kernels for 33%

profile of v1, /device:TPU:1, one launch (start us, length us, event | category | flops | bytes accessed | tf_op | source)
XLA Modules:
  0.0 220.3 jit_solution(5149148222335330759)
XLA Ops:
  0.6 22.6 %attention_forward.1 = (bf16[1024,768]{1,0:T(8,128)(2,1)}, bf16[1024,384]{1,0:T(8,128)(2,1)}, bf16[1024,384]{1,0:T(8,128)(2,1)}, bf16[1024,384]{1,0:T(8,128)(2,1...) custom-call(s32[1,8]{1,0:T(1,128)} %lens.3, ...), custom_call_target="tpu_custom_call" | custom-call | flops 4227858432 | bytes 16777216 | tf_op jit(solution)/shard_map/attention_forward/pallas_call | solution.py:218
  23.4 3.6 %collective-permute-done.part_b = bf16[1024,768]{1,0:T(8,128)(2,1)S(1)} collective-permute-done((bf16[1024,768]{1,0:T(8,128)(2,1)}, bf16[1024,768]{1,0:T(8,128)(2,1)S(1)}, u32[]{:S(2)}, u32[]{:S(2)}) %collective-permute-start) | collective-permute-done | bytes 1572896 | tf_op jit(solution)/shard_map/ppermute | solution.py:736
  28.1 16.8 %feed_forward.1 = (f32[1024,768]{1,0:T(8,128)}, bf16[1024,768]{1,0:T(8,128)(2,1)}, bf16[1024,1536]{1,0:T(8,128)(2,1)}, bf16[1024,1536]{1,0:T(8,128)(2,1)}, bf16[...) custom-call(s32[1]{0:T(128)S(6)} %sub.83.half, bf16[1024,768]{1,0:T(8,128)(2,1)} %x.5, ...), custom_call_target="tpu_custom_call" | custom-call | flops 9663676416 | bytes 25165824 | tf_op jit(solution)/shard_map/feed_forward/pallas_call | solution.py:286
  45.1 2.6 %collective-permute-start.2 = (bf16[768,768]{1,0:T(8,128)(2,1)}, bf16[768,768]{1,0:T(8,128)(2,1)S(1)}, u32[]{:S(2)}, u32[]{:S(2)}) collective-permute-start(bf16[768,768]{1,0:T(8,128)(2,1)} %get-tuple-element.96), channel_id=1, source_target_pairs={{0,2},{1,5},{2,0},{3,7},{4,6},{5,1},{6,4},{7,3},{8,10},{9,13},{10,... | collective-permute-start | bytes 3538952 | tf_op jit(solution)/shard_map/ppermute | solution.py:661
  47.7 4.8 %grad_down.1 = bf16[768,768]{1,0:T(8,128)(2,1)} custom-call(s32[1]{0:T(128)} %bitcast.3.half.side, bf16[1024,1536]{1,0:T(8,128)(2,1)} %get-tuple-element.102.left.act, bf16[1024,768]{1,0:T(8,128)(2,1)} %g.3), custom_call_target="tpu_custom_call" | custom-call | flops 1207959552 | bytes 6291456 | tf_op jit(solution)/shard_map/grad_down/pallas_call | solution.py:316
  53.8 13.2 %second_norm_backward.1 = (f32[1024,768]{1,0:T(8,128)}, bf16[1024,384]{1,0:T(8,128)(2,1)}, f32[8,1024]{1,0:T(8,128)}, bf16[384,1920]{1,0:T(8,128)(2,1)}, bf16[384,1920]{1,0:T(8,128)(2,1)}, /*index=5*/f32[8,768]{1,0:T(8,128)}) custom-call(s32[1]{0:T(128)S(6)} %sub.82.half, f32[1024,768]{1,0:T(8,128)} %get-tuple-element.85.mid, ...), custom_call_target="tpu_custom_call" | custom-call | flops 1811939328 | bytes 20971520 | tf_op jit(solution)/shard_map/second_norm_backward/pallas_call | solution.py:387
  69.0 26.0 %attention_backward.1 = (bf16[1024,1280]{1,0:T(8,128)(2,1)}, bf16[384,1280]{1,0:T(8,128)(2,1)}, bf16[384,1280]{1,0:T(8,128)(2,1)}) custom-call(s32[1,8]{1,0:T(1,128)} %lens.3, s32[1]{0:T(128)S(6)} %sub.80.half, bf16[1024,384]{1,0:T(8,128)(2,1)} %get-tuple-element.75.q, bf16[1024,384]{1,0:T(8,128)(2,1)} %get-tuple-element.76.k, ...), custom_call_target="tpu_custom_call" | custom-call | flops 4026531840 | bytes 12582912 | tf_op jit(solution)/shard_map/attention_backward/pallas_call | solution.py:543
  96.8 6.4 %down_projection.1.fold_a = bf16[1024,768]{1,0:T(8,128)(2,1)} custom-call(bf16[1024,1536]{1,0:T(8,128)(2,1)} %get-tuple-element.102.left.act, bf16[1536,768]{1,0:T(8,128)(2,1)} %down.3), custom_call_target="tpu_custom_call" | custom-call | flops 7247757312 | bytes 25165824 | tf_op jit(solution)/shard_map/down_projection/pallas_call | solution.py:628
  104.6 2.5 %add_convert_fusion = (bf16[192,1920]{1,0:T(8,128)(2,1)S(1)}, bf16[192,1920]{1,0:T(8,128)(2,1)}) fusion(bf16[384,1920]{1,0:T(8,128)(2,1)} %collective-permute-done.4, s32[]{:T(128)S(6)} %select_n.371, bf16[384,1920]{1,0:T(8,128)(2,1)S(1)} %copy-done.3, s32[]{:T(128)S(6)} %select_n.367), kind=kLoop, calls=%fused_computation.1 | loop fusion | flops 2949120 | bytes 4423688 | tf_op jit(solution)/shard_map/convert_element_type | solution.py:669
  109.2 6.4 %first_norm_grad.1.part_a = bf16[1024,768]{1,0:T(8,128)(2,1)} custom-call(bf16[1024,1280]{1,0:T(8,128)(2,1)} %get-tuple-element.106.cat, bf16[3,768,384]{2,1,0:T(8,128)(2,1)} %wqkv.3, bf16[128,768]{1,0:T(8,128)(2,1)} %bitcast.14), custom_call_target="tpu_custom_call" | custom-call | flops 6039797760 | bytes 18874368 | tf_op jit(solution)/shard_map/first_norm_grad/pallas_call | solution.py:579
  115.8 2.3 %collective-permute-start.7 = (bf16[96,768]{1,0:T(8,128)(2,1)}, bf16[96,768]{1,0:T(8,128)(2,1)S(1)}, u32[]{:S(2)}, u32[]{:S(2)}) collective-permute-start(bf16[96,768]{1,0:T(8,128)(2,1)} %get-tuple-element.167), channel_id=1, source_target_pairs={{0,16},{1,17},{2,18},{3,19},{4,20},{5,21},{6,22},{7,23},{8,24},{9,... | collective-permute-start | bytes 442376 | tf_op jit(solution)/shard_map/ppermute | solution.py:661
  122.2 3.0 %collective-permute-done.7 = bf16[96,768]{1,0:T(8,128)(2,1)S(1)} collective-permute-done((bf16[96,768]{1,0:T(8,128)(2,1)}, bf16[96,768]{1,0:T(8,128)(2,1)S(1)}, u32[]{:S(2)}, u32[]{:S(2)}) %collective-permute-start.7) | collective-permute-done | bytes 147488 | tf_op jit(solution)/shard_map/ppermute | solution.py:661
  127.8 3.3 %collective-permute-start.12 = (bf16[48,1920]{1,0:T(8,128)(2,1)S(1)}, bf16[48,1920]{1,0:T(8,128)(2,1)S(1)}, u32[]{:S(2)}, u32[]{:S(2)}) collective-permute-start(bf16[48,1920]{1,0:T(8,128)(2,1)S(1)} %get-tuple-element.163), channel_id=1, source_target_pairs={{0,16},{1,17},{2,18},{3,19},{4,20},{5,21},{6,22},{7,23},{8,24},{9,... | collective-permute-start | bytes 552968 | tf_op jit(solution)/shard_map/ppermute | solution.py:661
  134.5 8.8 %first_norm_backward.1 = (f32[1024,768]{1,0:T(8,128)}, bf16[1024,768]{1,0:T(8,128)(2,1)}, f32[8,768]{1,0:T(8,128)}) custom-call(bf16[1024,768]{1,0:T(8,128)(2,1)} %x.5, bf16[1024,768]{1,0:T(8,128)(2,1)} %first_norm_grad.1.part_a, bf16[1024,768]{1,0:T(8,128)(2,1)} %collective-permute-done.10.part_b, f32[2,768]{1,0:T(2,128)} %gains.7, ...), custom_call_target="tpu_custom_call" | custom-call | flops 56623104 | bytes 62914560 | tf_op jit(solution)/shard_map/first_norm_backward/pallas_call | solution.py:609
  151.3 5.7 %collective-permute-done.16 = bf16[48,1920]{1,0:T(8,128)(2,1)S(1)} collective-permute-done((bf16[48,1920]{1,0:T(8,128)(2,1)S(1)}, bf16[48,1920]{1,0:T(8,128)(2,1)S(1)}, u32[]{:S(2)}, u32[]{:S(2)}) %collective-permute-start.16) | collective-permute-done | bytes 184352 | tf_op jit(solution)/shard_map/ppermute | solution.py:661
  160.4 3.4 %collective-permute-done.19 = bf16[96,1920]{1,0:T(8,128)(2,1)S(1)} collective-permute-done((bf16[96,1920]{1,0:T(8,128)(2,1)S(1)}, bf16[96,1920]{1,0:T(8,128)(2,1)S(1)}, u32[]{:S(2)}, u32[]{:S(2)}) %collective-permute-start.19) | collective-permute-done | bytes 368672 | tf_op jit(solution)/shard_map/ppermute | solution.py:661
  165.6 2.8 %collective-permute-done.21 = bf16[48,1280]{1,0:T(8,128)(2,1)S(1)} collective-permute-done((bf16[48,1280]{1,0:T(8,128)(2,1)S(1)}, bf16[48,1280]{1,0:T(8,128)(2,1)S(1)}, u32[]{:S(2)}, u32[]{:S(2)}) %collective-permute-start.21) | collective-permute-done | bytes 122912 | tf_op jit(solution)/shard_map/ppermute | solution.py:661
  169.6 10.9 %collective-permute-done.23 = bf16[192,1920]{1,0:T(8,128)(2,1)S(1)} collective-permute-done((bf16[192,1920]{1,0:T(8,128)(2,1)S(1)}, bf16[192,1920]{1,0:T(8,128)(2,1)S(1)}, u32[]{:S(2)}, u32[]{:S(2)}) %collective-permute-start.23) | collective-permute-done | bytes 737312 | tf_op jit(solution)/shard_map/ppermute | solution.py:661
  182.7 11.4 %collective-permute-done.26 = bf16[192,1280]{1,0:T(8,128)(2,1)S(1)} collective-permute-done((bf16[192,1280]{1,0:T(8,128)(2,1)S(1)}, bf16[192,1280]{1,0:T(8,128)(2,1)S(1)}, u32[]{:S(2)}, u32[]{:S(2)}) %collective-permute-start.26) | collective-permute-done | bytes 491552 | tf_op jit(solution)/shard_map/ppermute | solution.py:661
  194.6 2.9 %collective-permute-done.27 = f32[2,768]{1,0:T(2,128)S(1)} collective-permute-done((f32[2,768]{1,0:T(2,128)S(1)}, f32[2,768]{1,0:T(2,128)S(1)}, u32[]{:S(2)}, u32[]{:S(2)}) %collective-permute-start.27) | collective-permute-done | bytes 6176 | tf_op jit(solution)/shard_map/ppermute | solution.py:661
  197.5 3.6 %collective-permute-done.28.other = bf16[768,768]{1,0:T(8,128)(2,1)S(1)} collective-permute-done((bf16[768,768]{1,0:T(8,128)(2,1)S(1)}, bf16[768,768]{1,0:T(8,128)(2,1)S(1)}, u32[]{:S(2)}, u32[]{:S(2)}) %collective-permute-start.28) | collective-permute-done | bytes 1179680 | tf_op jit(solution)/shard_map/ppermute | solution.py:661
  201.1 3.1 %join_halves.1 = f32[1536,768]{1,0:T(8,128)} custom-call(s32[1]{0:T(128)} %bitcast.3.half.side, bf16[768,768]{1,0:T(8,128)(2,1)S(1)} %pad_maximum_fusion.1.mine, bf16[768,768]{1,0:T(8,128)(2,1)S(1)} %collective-permute-done.28.other), custom_call_target="tpu_custom_call" | custom-call | bytes 21233664 | tf_op jit(solution)/shard_map/join_halves/pallas_call | solution.py:753
  204.1 5.5 %collective-permute-done.29 = f32[2,768]{1,0:T(2,128)S(1)} collective-permute-done((f32[2,768]{1,0:T(2,128)S(1)}, f32[2,768]{1,0:T(2,128)S(1)}, u32[]{:S(2)}, u32[]{:S(2)}) %collective-permute-start.29) | collective-permute-done | bytes 6176 | tf_op jit(solution)/shard_map/ppermute | solution.py:661
  216.6 2.8 %join_up.1 = (f32[768,1536]{1,0:T(8,128)}, f32[384,768]{1,0:T(8,128)}) custom-call(s32[1]{0:T(128)} %bitcast.2.side, bf16[384,1920]{1,0:T(8,128)(2,1)S(1)} %pad_maximum_fusion.mine, bf16[384,1920]{1,0:T(8,128)(2,1)S(1)} %collective-permute-done.31.other), custom_call_target="tpu_custom_call" | custom-call | bytes 26542080 | tf_op jit(solution)/shard_map/join_up/pallas_call | solution.py:787
  (104 shorter events, 45.0 us)
Async XLA Ops:
  45.1 22.0 %collective-permute-start.2 = (bf16[768,768]{1,0:T(8,128)(2,1)}, bf16[768,768]{1,0:T(8,128)(2,1)S(1)}, u32[]{:S(2)}, u32[]{:S(2)}) collective-permute-start(bf16[768,768]{1,0:T(8,128)(2,1)} %get-tuple-element.96), channel_id=1, source_target_pairs={{0,2},{1,5},{2,0},{3,7},{4,6},{5,1},{6,4},{7,3},{8,10},{9,13},{10,... | collective-permute-start | bytes 3538952 | tf_op jit(solution)/shard_map/ppermute | solution.py:661
  67.0 37.6 %collective-permute-start.4 = (bf16[384,1920]{1,0:T(8,128)(2,1)}, bf16[384,1920]{1,0:T(8,128)(2,1)}, u32[]{:S(2)}, u32[]{:S(2)}) collective-permute-start(bf16[384,1920]{1,0:T(8,128)(2,1)} %get-tuple-element.104), channel_id=1, source_target_pairs={{0,8},{1,5},{2,10},{3,7},{4,12},{5,1},{6,14},{7,3},{8,0},{9,13},{1... | collective-permute-start | bytes 4423688 | tf_op jit(solution)/shard_map/ppermute | solution.py:661
  67.4 27.9 %collective-permute-start.3 = (bf16[384,768]{1,0:T(8,128)(2,1)S(1)}, bf16[384,768]{1,0:T(8,128)(2,1)S(1)}, u32[]{:S(2)}, u32[]{:S(2)}) collective-permute-start(bf16[384,768]{1,0:T(8,128)(2,1)S(1)} %get-tuple-element.145), channel_id=1, source_target_pairs={{0,4},{1,9},{2,6},{3,11},{4,0},{5,13},{6,2},{7,15},{8,12},{9,1},{1... | collective-permute-start | bytes 1769480 | tf_op jit(solution)/shard_map/ppermute | solution.py:661
  95.0 30.3 %collective-permute-start.8 = (bf16[384,1280]{1,0:T(8,128)(2,1)}, bf16[384,1280]{1,0:T(8,128)(2,1)}, u32[]{:S(2)}, u32[]{:S(2)}) collective-permute-start(bf16[384,1280]{1,0:T(8,128)(2,1)} %get-tuple-element.111), channel_id=1, source_target_pairs={{0,2},{1,9},{2,0},{3,11},{4,6},{5,13},{6,4},{7,15},{8,10},{9,1},{1... | collective-permute-start | bytes 2949128 | tf_op jit(solution)/shard_map/ppermute | solution.py:661
  95.5 12.9 %collective-permute-start.5 = (bf16[192,768]{1,0:T(8,128)(2,1)S(1)}, bf16[192,768]{1,0:T(8,128)(2,1)S(1)}, u32[]{:S(2)}, u32[]{:S(2)}) collective-permute-start(bf16[192,768]{1,0:T(8,128)(2,1)S(1)} %get-tuple-element.155), channel_id=1, source_target_pairs={{0,8},{1,3},{2,10},{3,1},{4,12},{5,7},{6,14},{7,5},{8,0},{9,11},{1... | collective-permute-start | bytes 884744 | tf_op jit(solution)/shard_map/ppermute | solution.py:661
  103.1 30.2 %collective-permute-start.11 = (bf16[1024,768]{1,0:T(8,128)(2,1)}, bf16[1024,768]{1,0:T(8,128)(2,1)S(1)}, u32[]{:S(2)}, u32[]{:S(2)}) collective-permute-start(bf16[1024,768]{1,0:T(8,128)(2,1)} %down_projection.1.fold_a), channel_id=1, source_target_pairs={{0,1},{1,0},{2,3},{3,2},{4,5},{5,4},{6,7},{7,6},{8,9},{9,8},{10,11... | collective-permute-start | bytes 4718600 | tf_op jit(solution)/shard_map/ppermute | solution.py:736
  107.1 12.5 %collective-permute-start.6 = (bf16[192,1920]{1,0:T(8,128)(2,1)}, bf16[192,1920]{1,0:T(8,128)(2,1)}, u32[]{:S(2)}, u32[]{:S(2)}) collective-permute-start(bf16[192,1920]{1,0:T(8,128)(2,1)} %get-tuple-element.143), channel_id=1, source_target_pairs={{0,2},{1,9},{2,0},{3,11},{4,6},{5,13},{6,4},{7,15},{8,10},{9,1},{1... | collective-permute-start | bytes 2211848 | tf_op jit(solution)/shard_map/ppermute | solution.py:661
  115.6 17.7 %collective-permute-start.10 = (bf16[1024,768]{1,0:T(8,128)(2,1)}, bf16[1024,768]{1,0:T(8,128)(2,1)}, u32[]{:S(2)}, u32[]{:S(2)}) collective-permute-start(bf16[1024,768]{1,0:T(8,128)(2,1)} %first_norm_grad.1.part_a), channel_id=1, source_target_pairs={{0,1},{1,0},{2,3},{3,2},{4,5},{5,4},{6,7},{7,6},{8,9},{9,8},{10,11... | collective-permute-start | bytes 4718600 | tf_op jit(solution)/shard_map/ppermute | solution.py:736
  127.8 15.5 %collective-permute-start.12 = (bf16[48,1920]{1,0:T(8,128)(2,1)S(1)}, bf16[48,1920]{1,0:T(8,128)(2,1)S(1)}, u32[]{:S(2)}, u32[]{:S(2)}) collective-permute-start(bf16[48,1920]{1,0:T(8,128)(2,1)S(1)} %get-tuple-element.163), channel_id=1, source_target_pairs={{0,16},{1,17},{2,18},{3,19},{4,20},{5,21},{6,22},{7,23},{8,24},{9,... | collective-permute-start | bytes 552968 | tf_op jit(solution)/shard_map/ppermute | solution.py:661
  131.0 12.3 %collective-permute-start.13 = (bf16[192,1280]{1,0:T(8,128)(2,1)}, bf16[192,1280]{1,0:T(8,128)(2,1)S(1)}, u32[]{:S(2)}, u32[]{:S(2)}) collective-permute-start(bf16[192,1280]{1,0:T(8,128)(2,1)} %get-tuple-element.147), channel_id=1, source_target_pairs={{0,4},{1,3},{2,6},{3,1},{4,0},{5,7},{6,2},{7,5},{8,12},{9,11},{10,... | collective-permute-start | bytes 1474568 | tf_op jit(solution)/shard_map/ppermute | solution.py:661
  133.2 13.9 %collective-permute-start.14 = (bf16[96,768]{1,0:T(8,128)(2,1)S(1)}, bf16[96,768]{1,0:T(8,128)(2,1)S(1)}, u32[]{:S(2)}, u32[]{:S(2)}) collective-permute-start(bf16[96,768]{1,0:T(8,128)(2,1)S(1)} %add_convert_fusion.15), channel_id=1, source_target_pairs={{0,16},{1,17},{2,18},{3,19},{4,20},{5,21},{6,22},{7,23},{8,24},{9,... | collective-permute-start | bytes 442376 | tf_op jit(solution)/shard_map/ppermute | solution.py:661
  145.3 11.7 %collective-permute-start.16 = (bf16[48,1920]{1,0:T(8,128)(2,1)S(1)}, bf16[48,1920]{1,0:T(8,128)(2,1)S(1)}, u32[]{:S(2)}, u32[]{:S(2)}) collective-permute-start(bf16[48,1920]{1,0:T(8,128)(2,1)S(1)} %add_convert_fusion.12), channel_id=1, source_target_pairs={{0,16},{1,17},{2,18},{3,19},{4,20},{5,21},{6,22},{7,23},{8,24},{9,... | collective-permute-start | bytes 552968 | tf_op jit(solution)/shard_map/ppermute | solution.py:661
  147.2 10.9 %collective-permute-start.17 = (bf16[192,768]{1,0:T(8,128)(2,1)S(1)}, bf16[192,768]{1,0:T(8,128)(2,1)S(1)}, u32[]{:S(2)}, u32[]{:S(2)}) collective-permute-start(bf16[192,768]{1,0:T(8,128)(2,1)S(1)} %pad_maximum_fusion.7), channel_id=1, source_target_pairs={{0,8},{1,3},{2,10},{3,1},{4,12},{5,7},{6,14},{7,5},{8,0},{9,11},{1... | collective-permute-start | bytes 884744 | tf_op jit(solution)/shard_map/ppermute | solution.py:661
  148.2 15.8 %collective-permute-start.20 = (f32[2,768]{1,0:T(2,128)S(1)}, f32[2,768]{1,0:T(2,128)S(1)}, u32[]{:S(2)}, u32[]{:S(2)}) collective-permute-start(f32[2,768]{1,0:T(2,128)S(1)} %pad_maximum_fusion.9), channel_id=1, source_target_pairs={{0,2},{1,5},{2,0},{3,7},{4,6},{5,1},{6,4},{7,3},{8,10},{9,13},{10,... | collective-permute-start | bytes 18440 | tf_op jit(solution)/shard_map/ppermute | solution.py:661
  149.9 10.4 %collective-permute-start.18 = (bf16[48,1280]{1,0:T(8,128)(2,1)S(1)}, bf16[48,1280]{1,0:T(8,128)(2,1)S(1)}, u32[]{:S(2)}, u32[]{:S(2)}) collective-permute-start(bf16[48,1280]{1,0:T(8,128)(2,1)S(1)} %get-tuple-element.171), channel_id=1, source_target_pairs={{0,16},{1,17},{2,18},{3,19},{4,20},{5,21},{6,22},{7,23},{8,24},{9,... | collective-permute-start | bytes 368648 | tf_op jit(solution)/shard_map/ppermute | solution.py:661
  158.2 11.2 %collective-permute-start.22 = (bf16[384,768]{1,0:T(8,128)(2,1)S(1)}, bf16[384,768]{1,0:T(8,128)(2,1)S(1)}, u32[]{:S(2)}, u32[]{:S(2)}) collective-permute-start(bf16[384,768]{1,0:T(8,128)(2,1)S(1)} %pad_maximum_fusion.4), channel_id=1, source_target_pairs={{0,4},{1,9},{2,6},{3,11},{4,0},{5,13},{6,2},{7,15},{8,12},{9,1},{1... | collective-permute-start | bytes 1769480 | tf_op jit(solution)/shard_map/ppermute | solution.py:661
  163.9 16.5 %collective-permute-start.23 = (bf16[192,1920]{1,0:T(8,128)(2,1)S(1)}, bf16[192,1920]{1,0:T(8,128)(2,1)S(1)}, u32[]{:S(2)}, u32[]{:S(2)}) collective-permute-start(bf16[192,1920]{1,0:T(8,128)(2,1)S(1)} %pad_maximum_fusion.3), channel_id=1, source_target_pairs={{0,2},{1,9},{2,0},{3,11},{4,6},{5,13},{6,4},{7,15},{8,10},{9,1},{1... | collective-permute-start | bytes 2211848 | tf_op jit(solution)/shard_map/ppermute | solution.py:661
  164.0 16.7 %collective-permute-start.24 = (f32[2,768]{1,0:T(2,128)S(1)}, f32[2,768]{1,0:T(2,128)S(1)}, u32[]{:S(2)}, u32[]{:S(2)}) collective-permute-start(f32[2,768]{1,0:T(2,128)S(1)} %add.242), channel_id=1, source_target_pairs={{0,4},{1,9},{2,6},{3,11},{4,0},{5,13},{6,2},{7,15},{8,12},{9,1},{1... | collective-permute-start | bytes 18440 | tf_op jit(solution)/shard_map/ppermute | solution.py:661
  168.4 12.4 %collective-permute-start.25 = (bf16[96,1280]{1,0:T(8,128)(2,1)S(1)}, bf16[96,1280]{1,0:T(8,128)(2,1)S(1)}, u32[]{:S(2)}, u32[]{:S(2)}) collective-permute-start(bf16[96,1280]{1,0:T(8,128)(2,1)S(1)} %pad_maximum_fusion.8), channel_id=1, source_target_pairs={{0,8},{1,5},{2,10},{3,7},{4,12},{5,1},{6,14},{7,3},{8,0},{9,13},{1... | collective-permute-start | bytes 737288 | tf_op jit(solution)/shard_map/ppermute | solution.py:661
  180.8 13.3 %collective-permute-start.26 = (bf16[192,1280]{1,0:T(8,128)(2,1)S(1)}, bf16[192,1280]{1,0:T(8,128)(2,1)S(1)}, u32[]{:S(2)}, u32[]{:S(2)}) collective-permute-start(bf16[192,1280]{1,0:T(8,128)(2,1)S(1)} %pad_maximum_fusion.5), channel_id=1, source_target_pairs={{0,4},{1,3},{2,6},{3,1},{4,0},{5,7},{6,2},{7,5},{8,12},{9,11},{10,... | collective-permute-start | bytes 1474568 | tf_op jit(solution)/shard_map/ppermute | solution.py:661
  181.2 19.8 %collective-permute-start.28 = (bf16[768,768]{1,0:T(8,128)(2,1)S(1)}, bf16[768,768]{1,0:T(8,128)(2,1)S(1)}, u32[]{:S(2)}, u32[]{:S(2)}) collective-permute-start(bf16[768,768]{1,0:T(8,128)(2,1)S(1)} %pad_maximum_fusion.1.mine), channel_id=1, source_target_pairs={{0,2},{1,5},{2,0},{3,7},{4,6},{5,1},{6,4},{7,3},{8,10},{9,13},{10,... | collective-permute-start | bytes 3538952 | tf_op jit(solution)/shard_map/ppermute | solution.py:661
  181.9 34.7 %collective-permute-start.31 = (bf16[384,1920]{1,0:T(8,128)(2,1)S(1)}, bf16[384,1920]{1,0:T(8,128)(2,1)S(1)}, u32[]{:S(2)}, u32[]{:S(2)}) collective-permute-start(bf16[384,1920]{1,0:T(8,128)(2,1)S(1)} %pad_maximum_fusion.mine), channel_id=1, source_target_pairs={{0,8},{1,5},{2,10},{3,7},{4,12},{5,1},{6,14},{7,3},{8,0},{9,13},{1... | collective-permute-start | bytes 4423688 | tf_op jit(solution)/shard_map/ppermute | solution.py:661
  194.3 17.5 %collective-permute-start.30 = (bf16[384,1280]{1,0:T(8,128)(2,1)S(1)}, bf16[384,1280]{1,0:T(8,128)(2,1)S(1)}, u32[]{:S(2)}, u32[]{:S(2)}) collective-permute-start(bf16[384,1280]{1,0:T(8,128)(2,1)S(1)} %pad_maximum_fusion.2.mine), channel_id=1, source_target_pairs={{0,2},{1,9},{2,0},{3,11},{4,6},{5,13},{6,4},{7,15},{8,10},{9,1},{1... | collective-permute-start | bytes 2949128 | tf_op jit(solution)/shard_map/ppermute | solution.py:661
  197.5 12.2 %collective-permute-start.29 = (f32[2,768]{1,0:T(2,128)S(1)}, f32[2,768]{1,0:T(2,128)S(1)}, u32[]{:S(2)}, u32[]{:S(2)}) collective-permute-start(f32[2,768]{1,0:T(2,128)S(1)} %add.244), channel_id=1, source_target_pairs={{0,16},{1,17},{2,18},{3,19},{4,20},{5,21},{6,22},{7,23},{8,24},{9,... | collective-permute-start | bytes 18440 | tf_op jit(solution)/shard_map/ppermute | solution.py:661
  (15 other events, 92.6 us)

commit v2 on v1

--- a/solution.py
+++ b/solution.py
@@ -21,7 +21,7 @@
 UP = (2, 0, 1, 3), (1, 2, 0, 3)
 ATT = (0, 1, 2, 3), (2, 0, 1, 3)
 EARLY = "d"
-LATE = "dbudnudaufuadaudaugaddugaagdDagAgguU"
+LATE = "dbudnudaufuadaudaugadugaagDgAU"
 FREE = False
 
 SHARES = (3.0, 3.0, 3.0, 3.0, 3.0, 3.0)
@@ -140,13 +140,13 @@
     xf = x[...].astype(F32)
     h1 = (xf * norm_scale(xf) * gains[0:1, :]).astype(BF)
     h1_o[...] = h1
-    q32 = mm(h1, wqkv[0])
+    q32, k32, v32 = (mm(h1, wqkv[i]) for i in range(3))
+    sq32, sk32 = (mm_nt(h1, wsel_t[i]) for i in range(2))
     q = (q32.astype(BF) * scale).astype(BF)
     q_t = (q32.T.astype(BF) * scale).astype(BF)
-    k = mm(h1, wqkv[1]).astype(BF)
-    v32 = mm(h1, wqkv[2])
-    sq = (mm_nt(h1, wsel_t[0]).astype(BF) * scale).astype(BF)
-    sk = mm_nt(h1, wsel_t[1]).astype(BF)
+    k = k32.astype(BF)
+    sq = (sq32.astype(BF) * scale).astype(BF)
+    sk = sk32.astype(BF)
     q_o[...] = q
     k_o[...] = k
     v_o[...] = v32.astype(BF)
@@ -496,6 +496,7 @@
             dpen = both if dpen is None else dpen + both
             probs.append(prob.astype(BF))
             lows.append(dscore.astype(BF))
+        dpicked = split_dot(dpen, after) + carry
         for p in range(pairs):
             pair = slice(p * two, (p + 1) * two)
             for side in range(2):
@@ -505,7 +506,6 @@
                 )
             dv_s[:, pair] += mm(probs[p], dm_s[p, i])
             dk_s[:, pair] += mm(lows[p], qm_s[p, i])
-        dpicked = split_dot(dpen, after) + carry
         row = i * BLK + lax.broadcasted_iota(jnp.int32, (1, BLK), 1)
         chosen = (seg_j == seg_s[0:1, at]) & (col < row)
         dsel = jnp.where(chosen, -2.0 * dpicked * sel, 0.0).astype(BF)

time: 221 us -> 220 us (level)
  no operation moved by 1% of the time
where the time goes in v2:
time: 220 us; the launch traced here: 219 us
  Pallas kernels  112 us (51%)
  waiting for transfers between devices  60.3 us (27%)
  starting transfers between devices  31 us (14%)
  other arithmetic  9.26 us (4%)
  local copies, waits for them, and re-layouts  5.91 us (3%)
    ppermute x28, waiting for transfers between devices, swap(): return lax.ppermute(value, ('dp', 'tensor'), pairs)  56.7 us
    ppermute x28, starting transfers between devices, swap(): return lax.ppermute(value, ('dp', 'tensor'), pairs)  27.8 us
    pallas_call x1, Pallas kernels, backward(): pl.pallas_call(functools.partial(backward_kernel, n, heads), grid=(n,), i...  25.2 us
    pallas_call x1, Pallas kernels, forward(): pl.pallas_call(functools.partial(forward_kernel, heads), grid=(n,), in_sp...  22.6 us
    pallas_call x1, Pallas kernels, feed(): pl.pallas_call(feed_kernel, grid=(t // BLK,), in_specs=[smem(), rows(d),...  16.8 us
    pallas_call x1, Pallas kernels, middle(): pl.pallas_call(functools.partial(middle_kernel, hd), grid=(t // BLK,), in...  13.2 us
    pallas_call x1, Pallas kernels, finish(): pl.pallas_call(finish_kernel, grid=(t // BLK,), in_specs=[rows(d), rows(d...  8.81 us
    convert_element_type x9, other arithmetic, cut(): return (pieces[0].astype(F32) + pieces[1].astype(F32)).astype(BF)  7.48 us
  transfers between devices with their start and end apart: 33, of which 16 were waited for; matrix products, arithmetic and copies ran while one was open for 5% of the time, Pallas kernels for 33%

profile of v2, /device:TPU:1, one launch (start us, length us, event | category | flops | bytes accessed | tf_op | source)
XLA Modules:
  0.0 219.5 jit_solution(11421424775753547159)
XLA Ops:
  0.6 22.6 %attention_forward.1 = (bf16[1024,768]{1,0:T(8,128)(2,1)}, bf16[1024,384]{1,0:T(8,128)(2,1)}, bf16[1024,384]{1,0:T(8,128)(2,1)}, bf16[1024,384]{1,0:T(8,128)(2,1...) custom-call(s32[1,8]{1,0:T(1,128)} %lens.3, ...), custom_call_target="tpu_custom_call" | custom-call | flops 4227858432 | bytes 16777216 | tf_op jit(solution)/shard_map/attention_forward/pallas_call | solution.py:218
  23.4 3.6 %collective-permute-done.part_b = bf16[1024,768]{1,0:T(8,128)(2,1)S(1)} collective-permute-done((bf16[1024,768]{1,0:T(8,128)(2,1)}, bf16[1024,768]{1,0:T(8,128)(2,1)S(1)}, u32[]{:S(2)}, u32[]{:S(2)}) %collective-permute-start) | collective-permute-done | bytes 1572896 | tf_op jit(solution)/shard_map/ppermute | solution.py:736
  28.1 16.8 %feed_forward.1 = (f32[1024,768]{1,0:T(8,128)}, bf16[1024,768]{1,0:T(8,128)(2,1)}, bf16[1024,1536]{1,0:T(8,128)(2,1)}, bf16[1024,1536]{1,0:T(8,128)(2,1)}, bf16[...) custom-call(s32[1]{0:T(128)S(6)} %sub.83.half, bf16[1024,768]{1,0:T(8,128)(2,1)} %x.5, ...), custom_call_target="tpu_custom_call" | custom-call | flops 9663676416 | bytes 25165824 | tf_op jit(solution)/shard_map/feed_forward/pallas_call | solution.py:286
  45.1 2.6 %collective-permute-start.2 = (bf16[768,768]{1,0:T(8,128)(2,1)}, bf16[768,768]{1,0:T(8,128)(2,1)S(1)}, u32[]{:S(2)}, u32[]{:S(2)}) collective-permute-start(bf16[768,768]{1,0:T(8,128)(2,1)} %get-tuple-element.96), channel_id=1, source_target_pairs={{0,2},{1,5},{2,0},{3,7},{4,6},{5,1},{6,4},{7,3},{8,10},{9,13},{10,... | collective-permute-start | bytes 3538952 | tf_op jit(solution)/shard_map/ppermute | solution.py:661
  47.7 4.8 %grad_down.1 = bf16[768,768]{1,0:T(8,128)(2,1)} custom-call(s32[1]{0:T(128)} %bitcast.3.half.side, bf16[1024,1536]{1,0:T(8,128)(2,1)} %get-tuple-element.102.left.act, bf16[1024,768]{1,0:T(8,128)(2,1)} %g.3), custom_call_target="tpu_custom_call" | custom-call | flops 1207959552 | bytes 6291456 | tf_op jit(solution)/shard_map/grad_down/pallas_call | solution.py:316
  53.8 13.2 %second_norm_backward.1 = (f32[1024,768]{1,0:T(8,128)}, bf16[1024,384]{1,0:T(8,128)(2,1)}, f32[8,1024]{1,0:T(8,128)}, bf16[384,1920]{1,0:T(8,128)(2,1)}, bf16[384,1920]{1,0:T(8,128)(2,1)}, /*index=5*/f32[8,768]{1,0:T(8,128)}) custom-call(s32[1]{0:T(128)S(6)} %sub.82.half, f32[1024,768]{1,0:T(8,128)} %get-tuple-element.85.mid, ...), custom_call_target="tpu_custom_call" | custom-call | flops 1811939328 | bytes 20971520 | tf_op jit(solution)/shard_map/second_norm_backward/pallas_call | solution.py:387
  69.0 25.2 %attention_backward.1 = (bf16[1024,1280]{1,0:T(8,128)(2,1)}, bf16[384,1280]{1,0:T(8,128)(2,1)}, bf16[384,1280]{1,0:T(8,128)(2,1)}) custom-call(s32[1,8]{1,0:T(1,128)} %lens.3, s32[1]{0:T(128)S(6)} %sub.80.half, bf16[1024,384]{1,0:T(8,128)(2,1)} %get-tuple-element.75.q, bf16[1024,384]{1,0:T(8,128)(2,1)} %get-tuple-element.76.k, ...), custom_call_target="tpu_custom_call" | custom-call | flops 4026531840 | bytes 12582912 | tf_op jit(solution)/shard_map/attention_backward/pallas_call | solution.py:543
  96.0 6.4 %down_projection.1.fold_a = bf16[1024,768]{1,0:T(8,128)(2,1)} custom-call(bf16[1024,1536]{1,0:T(8,128)(2,1)} %get-tuple-element.102.left.act, bf16[1536,768]{1,0:T(8,128)(2,1)} %down.3), custom_call_target="tpu_custom_call" | custom-call | flops 7247757312 | bytes 25165824 | tf_op jit(solution)/shard_map/down_projection/pallas_call | solution.py:628
  103.8 2.5 %add_convert_fusion = (bf16[192,1920]{1,0:T(8,128)(2,1)S(1)}, bf16[192,1920]{1,0:T(8,128)(2,1)}) fusion(bf16[384,1920]{1,0:T(8,128)(2,1)} %collective-permute-done.4, s32[]{:T(128)S(6)} %select_n.371, bf16[384,1920]{1,0:T(8,128)(2,1)S(1)} %copy-done.3, s32[]{:T(128)S(6)} %select_n.367), kind=kLoop, calls=%fused_computation.1 | loop fusion | flops 2949120 | bytes 4423688 | tf_op jit(solution)/shard_map/convert_element_type | solution.py:669
  108.3 6.4 %first_norm_grad.1.part_a = bf16[1024,768]{1,0:T(8,128)(2,1)} custom-call(bf16[1024,1280]{1,0:T(8,128)(2,1)} %get-tuple-element.106.cat, bf16[3,768,384]{2,1,0:T(8,128)(2,1)} %wqkv.3, bf16[128,768]{1,0:T(8,128)(2,1)} %bitcast.14), custom_call_target="tpu_custom_call" | custom-call | flops 6039797760 | bytes 18874368 | tf_op jit(solution)/shard_map/first_norm_grad/pallas_call | solution.py:579
  115.0 2.3 %collective-permute-start.7 = (bf16[96,768]{1,0:T(8,128)(2,1)}, bf16[96,768]{1,0:T(8,128)(2,1)S(1)}, u32[]{:S(2)}, u32[]{:S(2)}) collective-permute-start(bf16[96,768]{1,0:T(8,128)(2,1)} %get-tuple-element.167), channel_id=1, source_target_pairs={{0,16},{1,17},{2,18},{3,19},{4,20},{5,21},{6,22},{7,23},{8,24},{9,... | collective-permute-start | bytes 442376 | tf_op jit(solution)/shard_map/ppermute | solution.py:661
  121.4 3.0 %collective-permute-done.7 = bf16[96,768]{1,0:T(8,128)(2,1)S(1)} collective-permute-done((bf16[96,768]{1,0:T(8,128)(2,1)}, bf16[96,768]{1,0:T(8,128)(2,1)S(1)}, u32[]{:S(2)}, u32[]{:S(2)}) %collective-permute-start.7) | collective-permute-done | bytes 147488 | tf_op jit(solution)/shard_map/ppermute | solution.py:661
  127.0 3.3 %collective-permute-start.12 = (bf16[48,1920]{1,0:T(8,128)(2,1)S(1)}, bf16[48,1920]{1,0:T(8,128)(2,1)S(1)}, u32[]{:S(2)}, u32[]{:S(2)}) collective-permute-start(bf16[48,1920]{1,0:T(8,128)(2,1)S(1)} %get-tuple-element.163), channel_id=1, source_target_pairs={{0,16},{1,17},{2,18},{3,19},{4,20},{5,21},{6,22},{7,23},{8,24},{9,... | collective-permute-start | bytes 552968 | tf_op jit(solution)/shard_map/ppermute | solution.py:661
  133.7 8.8 %first_norm_backward.1 = (f32[1024,768]{1,0:T(8,128)}, bf16[1024,768]{1,0:T(8,128)(2,1)}, f32[8,768]{1,0:T(8,128)}) custom-call(bf16[1024,768]{1,0:T(8,128)(2,1)} %x.5, bf16[1024,768]{1,0:T(8,128)(2,1)} %first_norm_grad.1.part_a, bf16[1024,768]{1,0:T(8,128)(2,1)} %collective-permute-done.10.part_b, f32[2,768]{1,0:T(2,128)} %gains.7, ...), custom_call_target="tpu_custom_call" | custom-call | flops 56623104 | bytes 62914560 | tf_op jit(solution)/shard_map/first_norm_backward/pallas_call | solution.py:609
  150.5 5.6 %collective-permute-done.16 = bf16[48,1920]{1,0:T(8,128)(2,1)S(1)} collective-permute-done((bf16[48,1920]{1,0:T(8,128)(2,1)S(1)}, bf16[48,1920]{1,0:T(8,128)(2,1)S(1)}, u32[]{:S(2)}, u32[]{:S(2)}) %collective-permute-start.16) | collective-permute-done | bytes 184352 | tf_op jit(solution)/shard_map/ppermute | solution.py:661
  159.5 3.5 %collective-permute-done.19 = bf16[96,1920]{1,0:T(8,128)(2,1)S(1)} collective-permute-done((bf16[96,1920]{1,0:T(8,128)(2,1)S(1)}, bf16[96,1920]{1,0:T(8,128)(2,1)S(1)}, u32[]{:S(2)}, u32[]{:S(2)}) %collective-permute-start.19) | collective-permute-done | bytes 368672 | tf_op jit(solution)/shard_map/ppermute | solution.py:661
  164.7 2.8 %collective-permute-done.21 = bf16[48,1280]{1,0:T(8,128)(2,1)S(1)} collective-permute-done((bf16[48,1280]{1,0:T(8,128)(2,1)S(1)}, bf16[48,1280]{1,0:T(8,128)(2,1)S(1)}, u32[]{:S(2)}, u32[]{:S(2)}) %collective-permute-start.21) | collective-permute-done | bytes 122912 | tf_op jit(solution)/shard_map/ppermute | solution.py:661
  168.8 10.9 %collective-permute-done.23 = bf16[192,1920]{1,0:T(8,128)(2,1)S(1)} collective-permute-done((bf16[192,1920]{1,0:T(8,128)(2,1)S(1)}, bf16[192,1920]{1,0:T(8,128)(2,1)S(1)}, u32[]{:S(2)}, u32[]{:S(2)}) %collective-permute-start.23) | collective-permute-done | bytes 737312 | tf_op jit(solution)/shard_map/ppermute | solution.py:661
  181.9 11.4 %collective-permute-done.26 = bf16[192,1280]{1,0:T(8,128)(2,1)S(1)} collective-permute-done((bf16[192,1280]{1,0:T(8,128)(2,1)S(1)}, bf16[192,1280]{1,0:T(8,128)(2,1)S(1)}, u32[]{:S(2)}, u32[]{:S(2)}) %collective-permute-start.26) | collective-permute-done | bytes 491552 | tf_op jit(solution)/shard_map/ppermute | solution.py:661
  193.8 2.9 %collective-permute-done.27 = f32[2,768]{1,0:T(2,128)S(1)} collective-permute-done((f32[2,768]{1,0:T(2,128)S(1)}, f32[2,768]{1,0:T(2,128)S(1)}, u32[]{:S(2)}, u32[]{:S(2)}) %collective-permute-start.27) | collective-permute-done | bytes 6176 | tf_op jit(solution)/shard_map/ppermute | solution.py:661
  196.7 3.6 %collective-permute-done.28.other = bf16[768,768]{1,0:T(8,128)(2,1)S(1)} collective-permute-done((bf16[768,768]{1,0:T(8,128)(2,1)S(1)}, bf16[768,768]{1,0:T(8,128)(2,1)S(1)}, u32[]{:S(2)}, u32[]{:S(2)}) %collective-permute-start.28) | collective-permute-done | bytes 1179680 | tf_op jit(solution)/shard_map/ppermute | solution.py:661
  200.2 3.1 %join_halves.1 = f32[1536,768]{1,0:T(8,128)} custom-call(s32[1]{0:T(128)} %bitcast.3.half.side, bf16[768,768]{1,0:T(8,128)(2,1)S(1)} %pad_maximum_fusion.1.mine, bf16[768,768]{1,0:T(8,128)(2,1)S(1)} %collective-permute-done.28.other), custom_call_target="tpu_custom_call" | custom-call | bytes 21233664 | tf_op jit(solution)/shard_map/join_halves/pallas_call | solution.py:753
  203.3 5.5 %collective-permute-done.29 = f32[2,768]{1,0:T(2,128)S(1)} collective-permute-done((f32[2,768]{1,0:T(2,128)S(1)}, f32[2,768]{1,0:T(2,128)S(1)}, u32[]{:S(2)}, u32[]{:S(2)}) %collective-permute-start.29) | collective-permute-done | bytes 6176 | tf_op jit(solution)/shard_map/ppermute | solution.py:661
  215.7 2.8 %join_up.1 = (f32[768,1536]{1,0:T(8,128)}, f32[384,768]{1,0:T(8,128)}) custom-call(s32[1]{0:T(128)} %bitcast.2.side, bf16[384,1920]{1,0:T(8,128)(2,1)S(1)} %pad_maximum_fusion.mine, bf16[384,1920]{1,0:T(8,128)(2,1)S(1)} %collective-permute-done.31.other), custom_call_target="tpu_custom_call" | custom-call | bytes 26542080 | tf_op jit(solution)/shard_map/join_up/pallas_call | solution.py:787
  (104 shorter events, 44.9 us)
Async XLA Ops:
  45.1 22.0 %collective-permute-start.2 = (bf16[768,768]{1,0:T(8,128)(2,1)}, bf16[768,768]{1,0:T(8,128)(2,1)S(1)}, u32[]{:S(2)}, u32[]{:S(2)}) collective-permute-start(bf16[768,768]{1,0:T(8,128)(2,1)} %get-tuple-element.96), channel_id=1, source_target_pairs={{0,2},{1,5},{2,0},{3,7},{4,6},{5,1},{6,4},{7,3},{8,10},{9,13},{10,... | collective-permute-start | bytes 3538952 | tf_op jit(solution)/shard_map/ppermute | solution.py:661
  67.0 36.8 %collective-permute-start.4 = (bf16[384,1920]{1,0:T(8,128)(2,1)}, bf16[384,1920]{1,0:T(8,128)(2,1)}, u32[]{:S(2)}, u32[]{:S(2)}) collective-permute-start(bf16[384,1920]{1,0:T(8,128)(2,1)} %get-tuple-element.104), channel_id=1, source_target_pairs={{0,8},{1,5},{2,10},{3,7},{4,12},{5,1},{6,14},{7,3},{8,0},{9,13},{1... | collective-permute-start | bytes 4423688 | tf_op jit(solution)/shard_map/ppermute | solution.py:661
  67.4 27.1 %collective-permute-start.3 = (bf16[384,768]{1,0:T(8,128)(2,1)S(1)}, bf16[384,768]{1,0:T(8,128)(2,1)S(1)}, u32[]{:S(2)}, u32[]{:S(2)}) collective-permute-start(bf16[384,768]{1,0:T(8,128)(2,1)S(1)} %get-tuple-element.145), channel_id=1, source_target_pairs={{0,4},{1,9},{2,6},{3,11},{4,0},{5,13},{6,2},{7,15},{8,12},{9,1},{1... | collective-permute-start | bytes 1769480 | tf_op jit(solution)/shard_map/ppermute | solution.py:661
  94.2 30.3 %collective-permute-start.8 = (bf16[384,1280]{1,0:T(8,128)(2,1)}, bf16[384,1280]{1,0:T(8,128)(2,1)}, u32[]{:S(2)}, u32[]{:S(2)}) collective-permute-start(bf16[384,1280]{1,0:T(8,128)(2,1)} %get-tuple-element.111), channel_id=1, source_target_pairs={{0,2},{1,9},{2,0},{3,11},{4,6},{5,13},{6,4},{7,15},{8,10},{9,1},{1... | collective-permute-start | bytes 2949128 | tf_op jit(solution)/shard_map/ppermute | solution.py:661
  94.7 12.9 %collective-permute-start.5 = (bf16[192,768]{1,0:T(8,128)(2,1)S(1)}, bf16[192,768]{1,0:T(8,128)(2,1)S(1)}, u32[]{:S(2)}, u32[]{:S(2)}) collective-permute-start(bf16[192,768]{1,0:T(8,128)(2,1)S(1)} %get-tuple-element.155), channel_id=1, source_target_pairs={{0,8},{1,3},{2,10},{3,1},{4,12},{5,7},{6,14},{7,5},{8,0},{9,11},{1... | collective-permute-start | bytes 884744 | tf_op jit(solution)/shard_map/ppermute | solution.py:661
  102.3 30.2 %collective-permute-start.11 = (bf16[1024,768]{1,0:T(8,128)(2,1)}, bf16[1024,768]{1,0:T(8,128)(2,1)S(1)}, u32[]{:S(2)}, u32[]{:S(2)}) collective-permute-start(bf16[1024,768]{1,0:T(8,128)(2,1)} %down_projection.1.fold_a), channel_id=1, source_target_pairs={{0,1},{1,0},{2,3},{3,2},{4,5},{5,4},{6,7},{7,6},{8,9},{9,8},{10,11... | collective-permute-start | bytes 4718600 | tf_op jit(solution)/shard_map/ppermute | solution.py:736
  106.3 12.5 %collective-permute-start.6 = (bf16[192,1920]{1,0:T(8,128)(2,1)}, bf16[192,1920]{1,0:T(8,128)(2,1)}, u32[]{:S(2)}, u32[]{:S(2)}) collective-permute-start(bf16[192,1920]{1,0:T(8,128)(2,1)} %get-tuple-element.143), channel_id=1, source_target_pairs={{0,2},{1,9},{2,0},{3,11},{4,6},{5,13},{6,4},{7,15},{8,10},{9,1},{1... | collective-permute-start | bytes 2211848 | tf_op jit(solution)/shard_map/ppermute | solution.py:661
  114.8 17.8 %collective-permute-start.10 = (bf16[1024,768]{1,0:T(8,128)(2,1)}, bf16[1024,768]{1,0:T(8,128)(2,1)}, u32[]{:S(2)}, u32[]{:S(2)}) collective-permute-start(bf16[1024,768]{1,0:T(8,128)(2,1)} %first_norm_grad.1.part_a), channel_id=1, source_target_pairs={{0,1},{1,0},{2,3},{3,2},{4,5},{5,4},{6,7},{7,6},{8,9},{9,8},{10,11... | collective-permute-start | bytes 4718600 | tf_op jit(solution)/shard_map/ppermute | solution.py:736
  127.0 15.5 %collective-permute-start.12 = (bf16[48,1920]{1,0:T(8,128)(2,1)S(1)}, bf16[48,1920]{1,0:T(8,128)(2,1)S(1)}, u32[]{:S(2)}, u32[]{:S(2)}) collective-permute-start(bf16[48,1920]{1,0:T(8,128)(2,1)S(1)} %get-tuple-element.163), channel_id=1, source_target_pairs={{0,16},{1,17},{2,18},{3,19},{4,20},{5,21},{6,22},{7,23},{8,24},{9,... | collective-permute-start | bytes 552968 | tf_op jit(solution)/shard_map/ppermute | solution.py:661
  130.2 12.3 %collective-permute-start.13 = (bf16[192,1280]{1,0:T(8,128)(2,1)}, bf16[192,1280]{1,0:T(8,128)(2,1)S(1)}, u32[]{:S(2)}, u32[]{:S(2)}) collective-permute-start(bf16[192,1280]{1,0:T(8,128)(2,1)} %get-tuple-element.147), channel_id=1, source_target_pairs={{0,4},{1,3},{2,6},{3,1},{4,0},{5,7},{6,2},{7,5},{8,12},{9,11},{10,... | collective-permute-start | bytes 1474568 | tf_op jit(solution)/shard_map/ppermute | solution.py:661
  132.4 13.9 %collective-permute-start.14 = (bf16[96,768]{1,0:T(8,128)(2,1)S(1)}, bf16[96,768]{1,0:T(8,128)(2,1)S(1)}, u32[]{:S(2)}, u32[]{:S(2)}) collective-permute-start(bf16[96,768]{1,0:T(8,128)(2,1)S(1)} %add_convert_fusion.15), channel_id=1, source_target_pairs={{0,16},{1,17},{2,18},{3,19},{4,20},{5,21},{6,22},{7,23},{8,24},{9,... | collective-permute-start | bytes 442376 | tf_op jit(solution)/shard_map/ppermute | solution.py:661
  144.5 11.7 %collective-permute-start.16 = (bf16[48,1920]{1,0:T(8,128)(2,1)S(1)}, bf16[48,1920]{1,0:T(8,128)(2,1)S(1)}, u32[]{:S(2)}, u32[]{:S(2)}) collective-permute-start(bf16[48,1920]{1,0:T(8,128)(2,1)S(1)} %add_convert_fusion.12), channel_id=1, source_target_pairs={{0,16},{1,17},{2,18},{3,19},{4,20},{5,21},{6,22},{7,23},{8,24},{9,... | collective-permute-start | bytes 552968 | tf_op jit(solution)/shard_map/ppermute | solution.py:661
  146.4 10.9 %collective-permute-start.17 = (bf16[192,768]{1,0:T(8,128)(2,1)S(1)}, bf16[192,768]{1,0:T(8,128)(2,1)S(1)}, u32[]{:S(2)}, u32[]{:S(2)}) collective-permute-start(bf16[192,768]{1,0:T(8,128)(2,1)S(1)} %pad_maximum_fusion.7), channel_id=1, source_target_pairs={{0,8},{1,3},{2,10},{3,1},{4,12},{5,7},{6,14},{7,5},{8,0},{9,11},{1... | collective-permute-start | bytes 884744 | tf_op jit(solution)/shard_map/ppermute | solution.py:661
  147.4 15.7 %collective-permute-start.20 = (f32[2,768]{1,0:T(2,128)S(1)}, f32[2,768]{1,0:T(2,128)S(1)}, u32[]{:S(2)}, u32[]{:S(2)}) collective-permute-start(f32[2,768]{1,0:T(2,128)S(1)} %pad_maximum_fusion.9), channel_id=1, source_target_pairs={{0,2},{1,5},{2,0},{3,7},{4,6},{5,1},{6,4},{7,3},{8,10},{9,13},{10,... | collective-permute-start | bytes 18440 | tf_op jit(solution)/shard_map/ppermute | solution.py:661
  149.1 10.3 %collective-permute-start.18 = (bf16[48,1280]{1,0:T(8,128)(2,1)S(1)}, bf16[48,1280]{1,0:T(8,128)(2,1)S(1)}, u32[]{:S(2)}, u32[]{:S(2)}) collective-permute-start(bf16[48,1280]{1,0:T(8,128)(2,1)S(1)} %get-tuple-element.171), channel_id=1, source_target_pairs={{0,16},{1,17},{2,18},{3,19},{4,20},{5,21},{6,22},{7,23},{8,24},{9,... | collective-permute-start | bytes 368648 | tf_op jit(solution)/shard_map/ppermute | solution.py:661
  157.4 11.2 %collective-permute-start.22 = (bf16[384,768]{1,0:T(8,128)(2,1)S(1)}, bf16[384,768]{1,0:T(8,128)(2,1)S(1)}, u32[]{:S(2)}, u32[]{:S(2)}) collective-permute-start(bf16[384,768]{1,0:T(8,128)(2,1)S(1)} %pad_maximum_fusion.4), channel_id=1, source_target_pairs={{0,4},{1,9},{2,6},{3,11},{4,0},{5,13},{6,2},{7,15},{8,12},{9,1},{1... | collective-permute-start | bytes 1769480 | tf_op jit(solution)/shard_map/ppermute | solution.py:661
  163.1 16.5 %collective-permute-start.23 = (bf16[192,1920]{1,0:T(8,128)(2,1)S(1)}, bf16[192,1920]{1,0:T(8,128)(2,1)S(1)}, u32[]{:S(2)}, u32[]{:S(2)}) collective-permute-start(bf16[192,1920]{1,0:T(8,128)(2,1)S(1)} %pad_maximum_fusion.3), channel_id=1, source_target_pairs={{0,2},{1,9},{2,0},{3,11},{4,6},{5,13},{6,4},{7,15},{8,10},{9,1},{1... | collective-permute-start | bytes 2211848 | tf_op jit(solution)/shard_map/ppermute | solution.py:661
  163.2 16.7 %collective-permute-start.24 = (f32[2,768]{1,0:T(2,128)S(1)}, f32[2,768]{1,0:T(2,128)S(1)}, u32[]{:S(2)}, u32[]{:S(2)}) collective-permute-start(f32[2,768]{1,0:T(2,128)S(1)} %add.242), channel_id=1, source_target_pairs={{0,4},{1,9},{2,6},{3,11},{4,0},{5,13},{6,2},{7,15},{8,12},{9,1},{1... | collective-permute-start | bytes 18440 | tf_op jit(solution)/shard_map/ppermute | solution.py:661
  167.6 12.4 %collective-permute-start.25 = (bf16[96,1280]{1,0:T(8,128)(2,1)S(1)}, bf16[96,1280]{1,0:T(8,128)(2,1)S(1)}, u32[]{:S(2)}, u32[]{:S(2)}) collective-permute-start(bf16[96,1280]{1,0:T(8,128)(2,1)S(1)} %pad_maximum_fusion.8), channel_id=1, source_target_pairs={{0,8},{1,5},{2,10},{3,7},{4,12},{5,1},{6,14},{7,3},{8,0},{9,13},{1... | collective-permute-start | bytes 737288 | tf_op jit(solution)/shard_map/ppermute | solution.py:661
  180.0 13.3 %collective-permute-start.26 = (bf16[192,1280]{1,0:T(8,128)(2,1)S(1)}, bf16[192,1280]{1,0:T(8,128)(2,1)S(1)}, u32[]{:S(2)}, u32[]{:S(2)}) collective-permute-start(bf16[192,1280]{1,0:T(8,128)(2,1)S(1)} %pad_maximum_fusion.5), channel_id=1, source_target_pairs={{0,4},{1,3},{2,6},{3,1},{4,0},{5,7},{6,2},{7,5},{8,12},{9,11},{10,... | collective-permute-start | bytes 1474568 | tf_op jit(solution)/shard_map/ppermute | solution.py:661
  180.4 19.8 %collective-permute-start.28 = (bf16[768,768]{1,0:T(8,128)(2,1)S(1)}, bf16[768,768]{1,0:T(8,128)(2,1)S(1)}, u32[]{:S(2)}, u32[]{:S(2)}) collective-permute-start(bf16[768,768]{1,0:T(8,128)(2,1)S(1)} %pad_maximum_fusion.1.mine), channel_id=1, source_target_pairs={{0,2},{1,5},{2,0},{3,7},{4,6},{5,1},{6,4},{7,3},{8,10},{9,13},{10,... | collective-permute-start | bytes 3538952 | tf_op jit(solution)/shard_map/ppermute | solution.py:661
  181.1 34.7 %collective-permute-start.31 = (bf16[384,1920]{1,0:T(8,128)(2,1)S(1)}, bf16[384,1920]{1,0:T(8,128)(2,1)S(1)}, u32[]{:S(2)}, u32[]{:S(2)}) collective-permute-start(bf16[384,1920]{1,0:T(8,128)(2,1)S(1)} %pad_maximum_fusion.mine), channel_id=1, source_target_pairs={{0,8},{1,5},{2,10},{3,7},{4,12},{5,1},{6,14},{7,3},{8,0},{9,13},{1... | collective-permute-start | bytes 4423688 | tf_op jit(solution)/shard_map/ppermute | solution.py:661
  193.5 17.6 %collective-permute-start.30 = (bf16[384,1280]{1,0:T(8,128)(2,1)S(1)}, bf16[384,1280]{1,0:T(8,128)(2,1)S(1)}, u32[]{:S(2)}, u32[]{:S(2)}) collective-permute-start(bf16[384,1280]{1,0:T(8,128)(2,1)S(1)} %pad_maximum_fusion.2.mine), channel_id=1, source_target_pairs={{0,2},{1,9},{2,0},{3,11},{4,6},{5,13},{6,4},{7,15},{8,10},{9,1},{1... | collective-permute-start | bytes 2949128 | tf_op jit(solution)/shard_map/ppermute | solution.py:661
  196.7 12.2 %collective-permute-start.29 = (f32[2,768]{1,0:T(2,128)S(1)}, f32[2,768]{1,0:T(2,128)S(1)}, u32[]{:S(2)}, u32[]{:S(2)}) collective-permute-start(f32[2,768]{1,0:T(2,128)S(1)} %add.244), channel_id=1, source_target_pairs={{0,16},{1,17},{2,18},{3,19},{4,20},{5,21},{6,22},{7,23},{8,24},{9,... | collective-permute-start | bytes 18440 | tf_op jit(solution)/shard_map/ppermute | solution.py:661
  (15 other events, 92.6 us)

commit v3 on v2

--- a/solution.py
+++ b/solution.py
@@ -806,7 +806,7 @@
     def put(piece):
         for i in range(3):
             qkv_o[i] = piece[:, i * wh : (i + 1) * wh].astype(F32)
-        sel_o[...] = piece[:, 3 * wh :].astype(F32)
+        sel_o[...] = piece[:, 3 * wh :].astype(F32).T
 
     pl.when(pl.program_id(0) == 0)(lambda: put(mine[...]))
     pl.when(pl.program_id(0) == 1)(lambda: put(other[...]))
@@ -823,10 +823,10 @@
             in_specs=[pl.BlockSpec((r, n), lambda s, side: (0, 0))] * 2,
             out_specs=[
                 pl.BlockSpec((3, r, wh), lambda s, side: (0, place(s, side), 0)),
-                pl.BlockSpec((r, 2 * hd), lambda s, side: (place(s, side), 0)),
+                pl.BlockSpec((2 * hd, r), lambda s, side: (0, place(s, side))),
             ],
         ),
-        out_shape=[shape((3, 2 * r, wh), F32), shape((2 * r, 2 * hd), F32)],
+        out_shape=[shape((3, 2 * r, wh), F32), shape((2 * hd, 2 * r), F32)],
         compiler_params=params(32),
         cost_estimate=cost(0, 12 * r * n, share=SHARES[5]),
         name="join_attention",
@@ -929,8 +929,7 @@
     gains = gains[0]
     grad_up, grad_out = done["up"]
     grad_qkv, select_part = done["att"]
-    select_t_sum = select_part.T
-    select_t_sum = select_t_sum + swap(select_t_sum)
+    select_t_sum = select_part + swap(select_part)
     grad_select = jnp.swapaxes(select_t_sum.reshape(2, hd, d), 1, 2)
     return (output, grad_inputs, grad_qkv, grad_out, grad_up, grad_down, grad_select, gains)
 

time: 220 us -> 220 us (level)
  no operation moved by 1% of the time
where the time goes in v3:
time: 220 us; the launch traced here: 219 us
  Pallas kernels  112 us (51%)
  waiting for transfers between devices  60.3 us (27%)
  starting transfers between devices  31 us (14%)
  other arithmetic  10 us (5%)
  local copies, waits for them, and re-layouts  5 us (2%)
    ppermute x28, waiting for transfers between devices, swap(): return lax.ppermute(value, ('dp', 'tensor'), pairs)  56.7 us
    ppermute x28, starting transfers between devices, swap(): return lax.ppermute(value, ('dp', 'tensor'), pairs)  27.8 us
    pallas_call x1, Pallas kernels, backward(): pl.pallas_call(functools.partial(backward_kernel, n, heads), grid=(n,), i...  25.2 us
    pallas_call x1, Pallas kernels, forward(): pl.pallas_call(functools.partial(forward_kernel, heads), grid=(n,), in_sp...  22.6 us
    pallas_call x1, Pallas kernels, feed(): pl.pallas_call(feed_kernel, grid=(t // BLK,), in_specs=[smem(), rows(d),...  16.8 us
    pallas_call x1, Pallas kernels, middle(): pl.pallas_call(functools.partial(middle_kernel, hd), grid=(t // BLK,), in...  13.2 us
    pallas_call x1, Pallas kernels, finish(): pl.pallas_call(finish_kernel, grid=(t // BLK,), in_specs=[rows(d), rows(d...  8.81 us
    convert_element_type x9, other arithmetic, cut(): return (pieces[0].astype(F32) + pieces[1].astype(F32)).astype(BF)  7.48 us
  transfers between devices with their start and end apart: 33, of which 16 were waited for; matrix products, arithmetic and copies ran while one was open for 5% of the time, Pallas kernels for 33%

profile of v3, /device:TPU:1, one launch (start us, length us, event | category | flops | bytes accessed | tf_op | source)
XLA Modules:
  0.0 219.3 jit_solution(16809657729692420427)
XLA Ops:
  0.6 22.6 %attention_forward.1 = (bf16[1024,768]{1,0:T(8,128)(2,1)}, bf16[1024,384]{1,0:T(8,128)(2,1)}, bf16[1024,384]{1,0:T(8,128)(2,1)}, bf16[1024,384]{1,0:T(8,128)(2,1...) custom-call(s32[1,8]{1,0:T(1,128)} %lens.3, ...), custom_call_target="tpu_custom_call" | custom-call | flops 4227858432 | bytes 16777216 | tf_op jit(solution)/shard_map/attention_forward/pallas_call | solution.py:218
  23.4 3.6 %collective-permute-done.part_b = bf16[1024,768]{1,0:T(8,128)(2,1)S(1)} collective-permute-done((bf16[1024,768]{1,0:T(8,128)(2,1)}, bf16[1024,768]{1,0:T(8,128)(2,1)S(1)}, u32[]{:S(2)}, u32[]{:S(2)}) %collective-permute-start) | collective-permute-done | bytes 1572896 | tf_op jit(solution)/shard_map/ppermute | solution.py:736
  28.1 16.8 %feed_forward.1 = (f32[1024,768]{1,0:T(8,128)}, bf16[1024,768]{1,0:T(8,128)(2,1)}, bf16[1024,1536]{1,0:T(8,128)(2,1)}, bf16[1024,1536]{1,0:T(8,128)(2,1)}, bf16[...) custom-call(s32[1]{0:T(128)S(6)} %sub.83.half, bf16[1024,768]{1,0:T(8,128)(2,1)} %x.5, ...), custom_call_target="tpu_custom_call" | custom-call | flops 9663676416 | bytes 25165824 | tf_op jit(solution)/shard_map/feed_forward/pallas_call | solution.py:286
  45.1 2.6 %collective-permute-start.2 = (bf16[768,768]{1,0:T(8,128)(2,1)}, bf16[768,768]{1,0:T(8,128)(2,1)S(1)}, u32[]{:S(2)}, u32[]{:S(2)}) collective-permute-start(bf16[768,768]{1,0:T(8,128)(2,1)} %get-tuple-element.96), channel_id=1, source_target_pairs={{0,2},{1,5},{2,0},{3,7},{4,6},{5,1},{6,4},{7,3},{8,10},{9,13},{10,... | collective-permute-start | bytes 3538952 | tf_op jit(solution)/shard_map/ppermute | solution.py:661
  47.7 4.8 %grad_down.1 = bf16[768,768]{1,0:T(8,128)(2,1)} custom-call(s32[1]{0:T(128)} %bitcast.3.half.side, bf16[1024,1536]{1,0:T(8,128)(2,1)} %get-tuple-element.102.left.act, bf16[1024,768]{1,0:T(8,128)(2,1)} %g.3), custom_call_target="tpu_custom_call" | custom-call | flops 1207959552 | bytes 6291456 | tf_op jit(solution)/shard_map/grad_down/pallas_call | solution.py:316
  53.8 13.2 %second_norm_backward.1 = (f32[1024,768]{1,0:T(8,128)}, bf16[1024,384]{1,0:T(8,128)(2,1)}, f32[8,1024]{1,0:T(8,128)}, bf16[384,1920]{1,0:T(8,128)(2,1)}, bf16[384,1920]{1,0:T(8,128)(2,1)}, /*index=5*/f32[8,768]{1,0:T(8,128)}) custom-call(s32[1]{0:T(128)S(6)} %sub.82.half, f32[1024,768]{1,0:T(8,128)} %get-tuple-element.85.mid, ...), custom_call_target="tpu_custom_call" | custom-call | flops 1811939328 | bytes 20971520 | tf_op jit(solution)/shard_map/second_norm_backward/pallas_call | solution.py:387
  69.0 25.2 %attention_backward.1 = (bf16[1024,1280]{1,0:T(8,128)(2,1)}, bf16[384,1280]{1,0:T(8,128)(2,1)}, bf16[384,1280]{1,0:T(8,128)(2,1)}) custom-call(s32[1,8]{1,0:T(1,128)} %lens.3, s32[1]{0:T(128)S(6)} %sub.80.half, bf16[1024,384]{1,0:T(8,128)(2,1)} %get-tuple-element.75.q, bf16[1024,384]{1,0:T(8,128)(2,1)} %get-tuple-element.76.k, ...), custom_call_target="tpu_custom_call" | custom-call | flops 4026531840 | bytes 12582912 | tf_op jit(solution)/shard_map/attention_backward/pallas_call | solution.py:543
  96.0 6.4 %down_projection.1.fold_a = bf16[1024,768]{1,0:T(8,128)(2,1)} custom-call(bf16[1024,1536]{1,0:T(8,128)(2,1)} %get-tuple-element.102.left.act, bf16[1536,768]{1,0:T(8,128)(2,1)} %down.3), custom_call_target="tpu_custom_call" | custom-call | flops 7247757312 | bytes 25165824 | tf_op jit(solution)/shard_map/down_projection/pallas_call | solution.py:628
  103.8 2.5 %add_convert_fusion = (bf16[192,1920]{1,0:T(8,128)(2,1)S(1)}, bf16[192,1920]{1,0:T(8,128)(2,1)}) fusion(bf16[384,1920]{1,0:T(8,128)(2,1)} %collective-permute-done.4, s32[]{:T(128)S(6)} %select_n.371, bf16[384,1920]{1,0:T(8,128)(2,1)S(1)} %copy-done.3, s32[]{:T(128)S(6)} %select_n.367), kind=kLoop, calls=%fused_computation.1 | loop fusion | flops 2949120 | bytes 4423688 | tf_op jit(solution)/shard_map/convert_element_type | solution.py:669
  108.3 6.4 %first_norm_grad.1.part_a = bf16[1024,768]{1,0:T(8,128)(2,1)} custom-call(bf16[1024,1280]{1,0:T(8,128)(2,1)} %get-tuple-element.106.cat, bf16[3,768,384]{2,1,0:T(8,128)(2,1)} %wqkv.3, bf16[128,768]{1,0:T(8,128)(2,1)} %bitcast.11), custom_call_target="tpu_custom_call" | custom-call | flops 6039797760 | bytes 18874368 | tf_op jit(solution)/shard_map/first_norm_grad/pallas_call | solution.py:579
  115.0 2.3 %collective-permute-start.7 = (bf16[96,768]{1,0:T(8,128)(2,1)}, bf16[96,768]{1,0:T(8,128)(2,1)S(1)}, u32[]{:S(2)}, u32[]{:S(2)}) collective-permute-start(bf16[96,768]{1,0:T(8,128)(2,1)} %get-tuple-element.167), channel_id=1, source_target_pairs={{0,16},{1,17},{2,18},{3,19},{4,20},{5,21},{6,22},{7,23},{8,24},{9,... | collective-permute-start | bytes 442376 | tf_op jit(solution)/shard_map/ppermute | solution.py:661
  121.4 3.0 %collective-permute-done.7 = bf16[96,768]{1,0:T(8,128)(2,1)S(1)} collective-permute-done((bf16[96,768]{1,0:T(8,128)(2,1)}, bf16[96,768]{1,0:T(8,128)(2,1)S(1)}, u32[]{:S(2)}, u32[]{:S(2)}) %collective-permute-start.7) | collective-permute-done | bytes 147488 | tf_op jit(solution)/shard_map/ppermute | solution.py:661
  127.0 3.3 %collective-permute-start.12 = (bf16[48,1920]{1,0:T(8,128)(2,1)S(1)}, bf16[48,1920]{1,0:T(8,128)(2,1)S(1)}, u32[]{:S(2)}, u32[]{:S(2)}) collective-permute-start(bf16[48,1920]{1,0:T(8,128)(2,1)S(1)} %get-tuple-element.163), channel_id=1, source_target_pairs={{0,16},{1,17},{2,18},{3,19},{4,20},{5,21},{6,22},{7,23},{8,24},{9,... | collective-permute-start | bytes 552968 | tf_op jit(solution)/shard_map/ppermute | solution.py:661
  133.7 8.8 %first_norm_backward.1 = (f32[1024,768]{1,0:T(8,128)}, bf16[1024,768]{1,0:T(8,128)(2,1)}, f32[8,768]{1,0:T(8,128)}) custom-call(bf16[1024,768]{1,0:T(8,128)(2,1)} %x.5, bf16[1024,768]{1,0:T(8,128)(2,1)} %first_norm_grad.1.part_a, bf16[1024,768]{1,0:T(8,128)(2,1)} %collective-permute-done.10.part_b, f32[2,768]{1,0:T(2,128)} %gains.7, ...), custom_call_target="tpu_custom_call" | custom-call | flops 56623104 | bytes 62914560 | tf_op jit(solution)/shard_map/first_norm_backward/pallas_call | solution.py:609
  150.5 5.6 %collective-permute-done.16 = bf16[48,1920]{1,0:T(8,128)(2,1)S(1)} collective-permute-done((bf16[48,1920]{1,0:T(8,128)(2,1)S(1)}, bf16[48,1920]{1,0:T(8,128)(2,1)S(1)}, u32[]{:S(2)}, u32[]{:S(2)}) %collective-permute-start.16) | collective-permute-done | bytes 184352 | tf_op jit(solution)/shard_map/ppermute | solution.py:661
  159.5 3.5 %collective-permute-done.19 = bf16[96,1920]{1,0:T(8,128)(2,1)S(1)} collective-permute-done((bf16[96,1920]{1,0:T(8,128)(2,1)S(1)}, bf16[96,1920]{1,0:T(8,128)(2,1)S(1)}, u32[]{:S(2)}, u32[]{:S(2)}) %collective-permute-start.19) | collective-permute-done | bytes 368672 | tf_op jit(solution)/shard_map/ppermute | solution.py:661
  164.7 2.8 %collective-permute-done.21 = bf16[48,1280]{1,0:T(8,128)(2,1)S(1)} collective-permute-done((bf16[48,1280]{1,0:T(8,128)(2,1)S(1)}, bf16[48,1280]{1,0:T(8,128)(2,1)S(1)}, u32[]{:S(2)}, u32[]{:S(2)}) %collective-permute-start.21) | collective-permute-done | bytes 122912 | tf_op jit(solution)/shard_map/ppermute | solution.py:661
  168.8 10.9 %collective-permute-done.23 = bf16[192,1920]{1,0:T(8,128)(2,1)S(1)} collective-permute-done((bf16[192,1920]{1,0:T(8,128)(2,1)S(1)}, bf16[192,1920]{1,0:T(8,128)(2,1)S(1)}, u32[]{:S(2)}, u32[]{:S(2)}) %collective-permute-start.23) | collective-permute-done | bytes 737312 | tf_op jit(solution)/shard_map/ppermute | solution.py:661
  181.9 11.4 %collective-permute-done.26 = bf16[192,1280]{1,0:T(8,128)(2,1)S(1)} collective-permute-done((bf16[192,1280]{1,0:T(8,128)(2,1)S(1)}, bf16[192,1280]{1,0:T(8,128)(2,1)S(1)}, u32[]{:S(2)}, u32[]{:S(2)}) %collective-permute-start.26) | collective-permute-done | bytes 491552 | tf_op jit(solution)/shard_map/ppermute | solution.py:661
  193.8 2.9 %collective-permute-done.27 = f32[2,768]{1,0:T(2,128)S(1)} collective-permute-done((f32[2,768]{1,0:T(2,128)S(1)}, f32[2,768]{1,0:T(2,128)S(1)}, u32[]{:S(2)}, u32[]{:S(2)}) %collective-permute-start.27) | collective-permute-done | bytes 6176 | tf_op jit(solution)/shard_map/ppermute | solution.py:661
  196.7 3.6 %collective-permute-done.28.other = bf16[768,768]{1,0:T(8,128)(2,1)S(1)} collective-permute-done((bf16[768,768]{1,0:T(8,128)(2,1)S(1)}, bf16[768,768]{1,0:T(8,128)(2,1)S(1)}, u32[]{:S(2)}, u32[]{:S(2)}) %collective-permute-start.28) | collective-permute-done | bytes 1179680 | tf_op jit(solution)/shard_map/ppermute | solution.py:661
  200.2 3.1 %join_halves.1 = f32[1536,768]{1,0:T(8,128)} custom-call(s32[1]{0:T(128)} %bitcast.3.half.side, bf16[768,768]{1,0:T(8,128)(2,1)S(1)} %pad_maximum_fusion.1.mine, bf16[768,768]{1,0:T(8,128)(2,1)S(1)} %collective-permute-done.28.other), custom_call_target="tpu_custom_call" | custom-call | bytes 21233664 | tf_op jit(solution)/shard_map/join_halves/pallas_call | solution.py:753
  203.3 5.5 %collective-permute-done.29 = f32[2,768]{1,0:T(2,128)S(1)} collective-permute-done((f32[2,768]{1,0:T(2,128)S(1)}, f32[2,768]{1,0:T(2,128)S(1)}, u32[]{:S(2)}, u32[]{:S(2)}) %collective-permute-start.29) | collective-permute-done | bytes 6176 | tf_op jit(solution)/shard_map/ppermute | solution.py:661
  215.7 2.8 %join_up.1 = (f32[768,1536]{1,0:T(8,128)}, f32[384,768]{1,0:T(8,128)}) custom-call(s32[1]{0:T(128)} %bitcast.2.side, bf16[384,1920]{1,0:T(8,128)(2,1)S(1)} %pad_maximum_fusion.mine, bf16[384,1920]{1,0:T(8,128)(2,1)S(1)} %collective-permute-done.31.other), custom_call_target="tpu_custom_call" | custom-call | bytes 26542080 | tf_op jit(solution)/shard_map/join_up/pallas_call | solution.py:787
  (103 shorter events, 44.7 us)
Async XLA Ops:
  45.1 22.0 %collective-permute-start.2 = (bf16[768,768]{1,0:T(8,128)(2,1)}, bf16[768,768]{1,0:T(8,128)(2,1)S(1)}, u32[]{:S(2)}, u32[]{:S(2)}) collective-permute-start(bf16[768,768]{1,0:T(8,128)(2,1)} %get-tuple-element.96), channel_id=1, source_target_pairs={{0,2},{1,5},{2,0},{3,7},{4,6},{5,1},{6,4},{7,3},{8,10},{9,13},{10,... | collective-permute-start | bytes 3538952 | tf_op jit(solution)/shard_map/ppermute | solution.py:661
  67.0 36.8 %collective-permute-start.4 = (bf16[384,1920]{1,0:T(8,128)(2,1)}, bf16[384,1920]{1,0:T(8,128)(2,1)}, u32[]{:S(2)}, u32[]{:S(2)}) collective-permute-start(bf16[384,1920]{1,0:T(8,128)(2,1)} %get-tuple-element.104), channel_id=1, source_target_pairs={{0,8},{1,5},{2,10},{3,7},{4,12},{5,1},{6,14},{7,3},{8,0},{9,13},{1... | collective-permute-start | bytes 4423688 | tf_op jit(solution)/shard_map/ppermute | solution.py:661
  67.4 27.1 %collective-permute-start.3 = (bf16[384,768]{1,0:T(8,128)(2,1)S(1)}, bf16[384,768]{1,0:T(8,128)(2,1)S(1)}, u32[]{:S(2)}, u32[]{:S(2)}) collective-permute-start(bf16[384,768]{1,0:T(8,128)(2,1)S(1)} %get-tuple-element.145), channel_id=1, source_target_pairs={{0,4},{1,9},{2,6},{3,11},{4,0},{5,13},{6,2},{7,15},{8,12},{9,1},{1... | collective-permute-start | bytes 1769480 | tf_op jit(solution)/shard_map/ppermute | solution.py:661
  94.2 30.3 %collective-permute-start.8 = (bf16[384,1280]{1,0:T(8,128)(2,1)}, bf16[384,1280]{1,0:T(8,128)(2,1)}, u32[]{:S(2)}, u32[]{:S(2)}) collective-permute-start(bf16[384,1280]{1,0:T(8,128)(2,1)} %get-tuple-element.111), channel_id=1, source_target_pairs={{0,2},{1,9},{2,0},{3,11},{4,6},{5,13},{6,4},{7,15},{8,10},{9,1},{1... | collective-permute-start | bytes 2949128 | tf_op jit(solution)/shard_map/ppermute | solution.py:661
  94.7 12.9 %collective-permute-start.5 = (bf16[192,768]{1,0:T(8,128)(2,1)S(1)}, bf16[192,768]{1,0:T(8,128)(2,1)S(1)}, u32[]{:S(2)}, u32[]{:S(2)}) collective-permute-start(bf16[192,768]{1,0:T(8,128)(2,1)S(1)} %get-tuple-element.155), channel_id=1, source_target_pairs={{0,8},{1,3},{2,10},{3,1},{4,12},{5,7},{6,14},{7,5},{8,0},{9,11},{1... | collective-permute-start | bytes 884744 | tf_op jit(solution)/shard_map/ppermute | solution.py:661
  102.3 30.2 %collective-permute-start.11 = (bf16[1024,768]{1,0:T(8,128)(2,1)}, bf16[1024,768]{1,0:T(8,128)(2,1)S(1)}, u32[]{:S(2)}, u32[]{:S(2)}) collective-permute-start(bf16[1024,768]{1,0:T(8,128)(2,1)} %down_projection.1.fold_a), channel_id=1, source_target_pairs={{0,1},{1,0},{2,3},{3,2},{4,5},{5,4},{6,7},{7,6},{8,9},{9,8},{10,11... | collective-permute-start | bytes 4718600 | tf_op jit(solution)/shard_map/ppermute | solution.py:736
  106.3 12.5 %collective-permute-start.6 = (bf16[192,1920]{1,0:T(8,128)(2,1)}, bf16[192,1920]{1,0:T(8,128)(2,1)}, u32[]{:S(2)}, u32[]{:S(2)}) collective-permute-start(bf16[192,1920]{1,0:T(8,128)(2,1)} %get-tuple-element.143), channel_id=1, source_target_pairs={{0,2},{1,9},{2,0},{3,11},{4,6},{5,13},{6,4},{7,15},{8,10},{9,1},{1... | collective-permute-start | bytes 2211848 | tf_op jit(solution)/shard_map/ppermute | solution.py:661
  114.8 17.8 %collective-permute-start.10 = (bf16[1024,768]{1,0:T(8,128)(2,1)}, bf16[1024,768]{1,0:T(8,128)(2,1)}, u32[]{:S(2)}, u32[]{:S(2)}) collective-permute-start(bf16[1024,768]{1,0:T(8,128)(2,1)} %first_norm_grad.1.part_a), channel_id=1, source_target_pairs={{0,1},{1,0},{2,3},{3,2},{4,5},{5,4},{6,7},{7,6},{8,9},{9,8},{10,11... | collective-permute-start | bytes 4718600 | tf_op jit(solution)/shard_map/ppermute | solution.py:736
  127.0 15.5 %collective-permute-start.12 = (bf16[48,1920]{1,0:T(8,128)(2,1)S(1)}, bf16[48,1920]{1,0:T(8,128)(2,1)S(1)}, u32[]{:S(2)}, u32[]{:S(2)}) collective-permute-start(bf16[48,1920]{1,0:T(8,128)(2,1)S(1)} %get-tuple-element.163), channel_id=1, source_target_pairs={{0,16},{1,17},{2,18},{3,19},{4,20},{5,21},{6,22},{7,23},{8,24},{9,... | collective-permute-start | bytes 552968 | tf_op jit(solution)/shard_map/ppermute | solution.py:661
  130.2 12.3 %collective-permute-start.13 = (bf16[192,1280]{1,0:T(8,128)(2,1)}, bf16[192,1280]{1,0:T(8,128)(2,1)S(1)}, u32[]{:S(2)}, u32[]{:S(2)}) collective-permute-start(bf16[192,1280]{1,0:T(8,128)(2,1)} %get-tuple-element.147), channel_id=1, source_target_pairs={{0,4},{1,3},{2,6},{3,1},{4,0},{5,7},{6,2},{7,5},{8,12},{9,11},{10,... | collective-permute-start | bytes 1474568 | tf_op jit(solution)/shard_map/ppermute | solution.py:661
  132.4 13.9 %collective-permute-start.14 = (bf16[96,768]{1,0:T(8,128)(2,1)S(1)}, bf16[96,768]{1,0:T(8,128)(2,1)S(1)}, u32[]{:S(2)}, u32[]{:S(2)}) collective-permute-start(bf16[96,768]{1,0:T(8,128)(2,1)S(1)} %add_convert_fusion.15), channel_id=1, source_target_pairs={{0,16},{1,17},{2,18},{3,19},{4,20},{5,21},{6,22},{7,23},{8,24},{9,... | collective-permute-start | bytes 442376 | tf_op jit(solution)/shard_map/ppermute | solution.py:661
  144.5 11.7 %collective-permute-start.16 = (bf16[48,1920]{1,0:T(8,128)(2,1)S(1)}, bf16[48,1920]{1,0:T(8,128)(2,1)S(1)}, u32[]{:S(2)}, u32[]{:S(2)}) collective-permute-start(bf16[48,1920]{1,0:T(8,128)(2,1)S(1)} %add_convert_fusion.12), channel_id=1, source_target_pairs={{0,16},{1,17},{2,18},{3,19},{4,20},{5,21},{6,22},{7,23},{8,24},{9,... | collective-permute-start | bytes 552968 | tf_op jit(solution)/shard_map/ppermute | solution.py:661
  146.4 10.9 %collective-permute-start.17 = (bf16[192,768]{1,0:T(8,128)(2,1)S(1)}, bf16[192,768]{1,0:T(8,128)(2,1)S(1)}, u32[]{:S(2)}, u32[]{:S(2)}) collective-permute-start(bf16[192,768]{1,0:T(8,128)(2,1)S(1)} %pad_maximum_fusion.7), channel_id=1, source_target_pairs={{0,8},{1,3},{2,10},{3,1},{4,12},{5,7},{6,14},{7,5},{8,0},{9,11},{1... | collective-permute-start | bytes 884744 | tf_op jit(solution)/shard_map/ppermute | solution.py:661
  147.4 15.7 %collective-permute-start.20 = (f32[2,768]{1,0:T(2,128)S(1)}, f32[2,768]{1,0:T(2,128)S(1)}, u32[]{:S(2)}, u32[]{:S(2)}) collective-permute-start(f32[2,768]{1,0:T(2,128)S(1)} %pad_maximum_fusion.9), channel_id=1, source_target_pairs={{0,2},{1,5},{2,0},{3,7},{4,6},{5,1},{6,4},{7,3},{8,10},{9,13},{10,... | collective-permute-start | bytes 18440 | tf_op jit(solution)/shard_map/ppermute | solution.py:661
  149.1 10.3 %collective-permute-start.18 = (bf16[48,1280]{1,0:T(8,128)(2,1)S(1)}, bf16[48,1280]{1,0:T(8,128)(2,1)S(1)}, u32[]{:S(2)}, u32[]{:S(2)}) collective-permute-start(bf16[48,1280]{1,0:T(8,128)(2,1)S(1)} %get-tuple-element.171), channel_id=1, source_target_pairs={{0,16},{1,17},{2,18},{3,19},{4,20},{5,21},{6,22},{7,23},{8,24},{9,... | collective-permute-start | bytes 368648 | tf_op jit(solution)/shard_map/ppermute | solution.py:661
  157.4 11.2 %collective-permute-start.22 = (bf16[384,768]{1,0:T(8,128)(2,1)S(1)}, bf16[384,768]{1,0:T(8,128)(2,1)S(1)}, u32[]{:S(2)}, u32[]{:S(2)}) collective-permute-start(bf16[384,768]{1,0:T(8,128)(2,1)S(1)} %pad_maximum_fusion.4), channel_id=1, source_target_pairs={{0,4},{1,9},{2,6},{3,11},{4,0},{5,13},{6,2},{7,15},{8,12},{9,1},{1... | collective-permute-start | bytes 1769480 | tf_op jit(solution)/shard_map/ppermute | solution.py:661
  163.1 16.5 %collective-permute-start.23 = (bf16[192,1920]{1,0:T(8,128)(2,1)S(1)}, bf16[192,1920]{1,0:T(8,128)(2,1)S(1)}, u32[]{:S(2)}, u32[]{:S(2)}) collective-permute-start(bf16[192,1920]{1,0:T(8,128)(2,1)S(1)} %pad_maximum_fusion.3), channel_id=1, source_target_pairs={{0,2},{1,9},{2,0},{3,11},{4,6},{5,13},{6,4},{7,15},{8,10},{9,1},{1... | collective-permute-start | bytes 2211848 | tf_op jit(solution)/shard_map/ppermute | solution.py:661
  163.2 16.7 %collective-permute-start.24 = (f32[2,768]{1,0:T(2,128)S(1)}, f32[2,768]{1,0:T(2,128)S(1)}, u32[]{:S(2)}, u32[]{:S(2)}) collective-permute-start(f32[2,768]{1,0:T(2,128)S(1)} %add.242), channel_id=1, source_target_pairs={{0,4},{1,9},{2,6},{3,11},{4,0},{5,13},{6,2},{7,15},{8,12},{9,1},{1... | collective-permute-start | bytes 18440 | tf_op jit(solution)/shard_map/ppermute | solution.py:661
  167.6 12.4 %collective-permute-start.25 = (bf16[96,1280]{1,0:T(8,128)(2,1)S(1)}, bf16[96,1280]{1,0:T(8,128)(2,1)S(1)}, u32[]{:S(2)}, u32[]{:S(2)}) collective-permute-start(bf16[96,1280]{1,0:T(8,128)(2,1)S(1)} %pad_maximum_fusion.8), channel_id=1, source_target_pairs={{0,8},{1,5},{2,10},{3,7},{4,12},{5,1},{6,14},{7,3},{8,0},{9,13},{1... | collective-permute-start | bytes 737288 | tf_op jit(solution)/shard_map/ppermute | solution.py:661
  180.0 13.3 %collective-permute-start.26 = (bf16[192,1280]{1,0:T(8,128)(2,1)S(1)}, bf16[192,1280]{1,0:T(8,128)(2,1)S(1)}, u32[]{:S(2)}, u32[]{:S(2)}) collective-permute-start(bf16[192,1280]{1,0:T(8,128)(2,1)S(1)} %pad_maximum_fusion.5), channel_id=1, source_target_pairs={{0,4},{1,3},{2,6},{3,1},{4,0},{5,7},{6,2},{7,5},{8,12},{9,11},{10,... | collective-permute-start | bytes 1474568 | tf_op jit(solution)/shard_map/ppermute | solution.py:661
  180.4 19.8 %collective-permute-start.28 = (bf16[768,768]{1,0:T(8,128)(2,1)S(1)}, bf16[768,768]{1,0:T(8,128)(2,1)S(1)}, u32[]{:S(2)}, u32[]{:S(2)}) collective-permute-start(bf16[768,768]{1,0:T(8,128)(2,1)S(1)} %pad_maximum_fusion.1.mine), channel_id=1, source_target_pairs={{0,2},{1,5},{2,0},{3,7},{4,6},{5,1},{6,4},{7,3},{8,10},{9,13},{10,... | collective-permute-start | bytes 3538952 | tf_op jit(solution)/shard_map/ppermute | solution.py:661
  181.1 34.7 %collective-permute-start.31 = (bf16[384,1920]{1,0:T(8,128)(2,1)S(1)}, bf16[384,1920]{1,0:T(8,128)(2,1)S(1)}, u32[]{:S(2)}, u32[]{:S(2)}) collective-permute-start(bf16[384,1920]{1,0:T(8,128)(2,1)S(1)} %pad_maximum_fusion.mine), channel_id=1, source_target_pairs={{0,8},{1,5},{2,10},{3,7},{4,12},{5,1},{6,14},{7,3},{8,0},{9,13},{1... | collective-permute-start | bytes 4423688 | tf_op jit(solution)/shard_map/ppermute | solution.py:661
  193.5 17.6 %collective-permute-start.30 = (bf16[384,1280]{1,0:T(8,128)(2,1)S(1)}, bf16[384,1280]{1,0:T(8,128)(2,1)S(1)}, u32[]{:S(2)}, u32[]{:S(2)}) collective-permute-start(bf16[384,1280]{1,0:T(8,128)(2,1)S(1)} %pad_maximum_fusion.2.mine), channel_id=1, source_target_pairs={{0,2},{1,9},{2,0},{3,11},{4,6},{5,13},{6,4},{7,15},{8,10},{9,1},{1... | collective-permute-start | bytes 2949128 | tf_op jit(solution)/shard_map/ppermute | solution.py:661
  196.7 12.2 %collective-permute-start.29 = (f32[2,768]{1,0:T(2,128)S(1)}, f32[2,768]{1,0:T(2,128)S(1)}, u32[]{:S(2)}, u32[]{:S(2)}) collective-permute-start(f32[2,768]{1,0:T(2,128)S(1)} %add.244), channel_id=1, source_target_pairs={{0,16},{1,17},{2,18},{3,19},{4,20},{5,21},{6,22},{7,23},{8,24},{9,... | collective-permute-start | bytes 18440 | tf_op jit(solution)/shard_map/ppermute | solution.py:661
  (15 other events, 92.6 us)
